TPU v7x, 32 devices: a whole 2x2x4 slice. The times are simulated.
32 devices in a mesh: grp: 8 (over z, x), mem: 4 (over y, core).
Axes of the slice: x: 2, y: 2, z: 4, core: 2. Of those that a mesh axis runs over, the one named last changes fastest.
Arguments:
- state: float32 [3, 128, 16, 128], P(None, ('grp', 'mem')), may hold values from -0.18 to 0.18
- direction: float32 [3, 128, 16, 128], P(None, ('grp', 'mem')), may hold values from -0.6 to 0.6
- rhs: float32 [3, 128, 16, 128], P(None, ('grp', 'mem')), may hold values from -6 to 6
- clamp: int32 [128, 16], P(('grp', 'mem')), may hold values 0 or 1
- stiffness: float32 [32, 4, 32], P(('grp', 'mem')), may hold values from 0.5 to 5
- coarse_owner: int32 [32, 128], P(('grp', 'mem')), may hold values from 0 to 127, as said below
- coarse_inverse: float32 [32, 2, 192, 192], P(('grp', 'mem')), may hold values from -0.006 to 0.006
Outputs:
- new_direction: float32 [3, 128, 16, 128], P(None, ('grp', 'mem'))
- residual: float32 [3, 128, 16, 128], P(None, ('grp', 'mem'))
- coarse_residual: float32 [3, 32, 4, 32], P(None, ('grp', 'mem'))
Inputs may be any that keep to these rules, and one draw needn't show every extreme that they name: `coarse_owner`: each layer's row is a permutation of 0 to 127.
All inputs are finite; a program needn't handle non-finite values. No bound on the sum of `clamp` on one device may be relied on, other than what follows from the above.
Results may differ from a plain program's by a relative error of at most 0.0003.
Values sent between devices are 32-bit elements; how exact they have to be, the bound alone decides.
A program may use at most 64 MiB of HBM per device.

v0:
```python
import jax
import jax.numpy as jnp
import numpy as np
from jax import lax
from jax.sharding import PartitionSpec as P

LAME_FIRST = 1.2
LAME_SHEAR = 0.8
HIGHEST = lax.Precision.HIGHEST


def shifted(block, axis, distance):
    devices = range(lax.axis_size(axis))
    route = [(i - distance, i) for i in devices if i - distance in devices]
    return lax.ppermute(block, axis, route)


def gauss_rule():
    inner = np.sqrt(5.0 - 2.0 * np.sqrt(10.0 / 7.0)) / 3.0
    outer = np.sqrt(5.0 + 2.0 * np.sqrt(10.0 / 7.0)) / 3.0
    inner_weight = (322.0 + 13.0 * np.sqrt(70.0)) / 900.0
    outer_weight = (322.0 - 13.0 * np.sqrt(70.0)) / 900.0
    points = np.array([-outer, -inner, 0.0, inner, outer])
    weights = np.array([outer_weight, inner_weight, 128.0 / 225.0, inner_weight, outer_weight])
    return (points, weights)


def basis_tables():
    gll_points = np.array([-1.0, -np.sqrt(3.0 / 7.0), 0.0, np.sqrt(3.0 / 7.0), 1.0])
    gauss_points, gauss_weights = gauss_rule()
    values = np.zeros((5, 5))
    slopes = np.zeros((5, 5))
    for j in range(5):
        others = [gll_points[k] for k in range(5) if k != j]
        denominator = np.prod([gll_points[j] - o for o in others])
        for q in range(5):
            t = gauss_points[q]
            values[q, j] = np.prod([t - o for o in others]) / denominator
            total = 0.0
            for i in range(4):
                total += np.prod([t - others[k] for k in range(4) if k != i])
            slopes[q, j] = 2.0 * total / denominator
    return (gll_points, gauss_weights, values, slopes)


def banded(table, count):
    banded_matrix = np.zeros((5 * count, 4 * count + 1))
    for e in range(count):
        banded_matrix[5 * e : 5 * e + 5, 4 * e : 4 * e + 5] = table
    return banded_matrix


def restrictor(gll_points, count):
    result = np.zeros((count, 4 * count))
    for e in range(count):
        for j in range(4):
            result[e, 4 * e + j] += (1.0 - gll_points[j]) / 2.0
            if e + 1 < count:
                result[e + 1, 4 * e + j] += (1.0 + gll_points[j]) / 2.0
    return result


def operators(count_y, count_z):
    gll_points, gauss_weights, values, slopes = basis_tables()
    return (
        jnp.asarray(values, jnp.float32),
        jnp.asarray(slopes, jnp.float32),
        jnp.asarray(banded(values, count_y), jnp.float32),
        jnp.asarray(banded(slopes, count_y), jnp.float32),
        jnp.asarray(banded(values, count_z), jnp.float32),
        jnp.asarray(banded(slopes, count_z), jnp.float32),
    )


def gradient(field, mats):
    basis_x, slope_x, basis_y, slope_y, basis_z, slope_z = mats
    along_b = jnp.einsum("cxyz,qz->cxyq", field, basis_z, precision=HIGHEST)
    along_d = jnp.einsum("cxyz,qz->cxyq", field, slope_z, precision=HIGHEST)
    plain_b = jnp.einsum("cxyq,py->cxpq", along_b, basis_y, precision=HIGHEST)
    sloped_b = jnp.einsum("cxyq,py->cxpq", along_b, slope_y, precision=HIGHEST)
    plain_d = jnp.einsum("cxyq,py->cxpq", along_d, basis_y, precision=HIGHEST)
    grad_x = jnp.einsum("cxpq,rx->crpq", plain_b, slope_x, precision=HIGHEST)
    grad_y = jnp.einsum("cxpq,rx->crpq", sloped_b, basis_x, precision=HIGHEST)
    grad_z = jnp.einsum("cxpq,rx->crpq", plain_d, basis_x, precision=HIGHEST)
    return (grad_x, grad_y, grad_z)


def divergence(fluxes, mats):
    basis_x, slope_x, basis_y, slope_y, basis_z, slope_z = mats
    part_x = jnp.einsum("crpq,rx->cxpq", fluxes[0], slope_x, precision=HIGHEST)
    part_y = jnp.einsum("crpq,rx->cxpq", fluxes[1], basis_x, precision=HIGHEST)
    part_z = jnp.einsum("crpq,rx->cxpq", fluxes[2], basis_x, precision=HIGHEST)
    side_b = jnp.einsum("cxpq,py->cxyq", part_x, basis_y, precision=HIGHEST) + jnp.einsum(
        "cxpq,py->cxyq", part_y, slope_y, precision=HIGHEST
    )
    side_d = jnp.einsum("cxpq,py->cxyq", part_z, basis_y, precision=HIGHEST)
    return jnp.einsum("cxyq,qz->cxyz", side_b, basis_z, precision=HIGHEST) + jnp.einsum(
        "cxyq,qz->cxyz", side_d, slope_z, precision=HIGHEST
    )


def state_terms(gradients):
    deform = [[gradients[a][c] + (1.0 if c == a else 0.0) for a in range(3)] for c in range(3)]
    strain = [
        [
            0.5
            * (
                deform[0][a] * deform[0][b]
                + deform[1][a] * deform[1][b]
                + deform[2][a] * deform[2][b]
            )
            - (0.5 if a == b else 0.0)
            for b in range(3)
        ]
        for a in range(3)
    ]
    strain_trace = strain[0][0] + strain[1][1] + strain[2][2]
    stress = [
        [
            2.0 * LAME_SHEAR * strain[a][b] + (LAME_FIRST * strain_trace if a == b else 0.0)
            for b in range(3)
        ]
        for a in range(3)
    ]
    return (deform, stress)


def tangent_flux(gradients, deform, stress, weighting):
    change = [[gradients[a][c] for a in range(3)] for c in range(3)]
    cross_terms = [
        [
            deform[0][a] * change[0][b] + deform[1][a] * change[1][b] + deform[2][a] * change[2][b]
            for b in range(3)
        ]
        for a in range(3)
    ]
    strain_change = [
        [0.5 * (cross_terms[a][b] + cross_terms[b][a]) for b in range(3)] for a in range(3)
    ]
    trace_change = strain_change[0][0] + strain_change[1][1] + strain_change[2][2]
    stress_change = [
        [
            2.0 * LAME_SHEAR * strain_change[a][b] + (LAME_FIRST * trace_change if a == b else 0.0)
            for b in range(3)
        ]
        for a in range(3)
    ]
    fluxes = []
    for a in range(3):
        rows_of = []
        for c in range(3):
            entry = (
                change[c][0] * stress[0][a]
                + change[c][1] * stress[1][a]
                + change[c][2] * stress[2][a]
                + deform[c][0] * stress_change[0][a]
                + deform[c][1] * stress_change[1][a]
                + deform[c][2] * stress_change[2][a]
            )
            rows_of.append(entry * weighting)
        fluxes.append(jnp.stack(rows_of))
    return fluxes


def quad_weighting(element_stiffness, gauss_weights):
    count_y, count_z = element_stiffness.shape
    spread = jnp.repeat(jnp.repeat(element_stiffness, 5, axis=0), 5, axis=1)
    weight_y = np.tile(gauss_weights, count_y)
    weight_z = np.tile(gauss_weights, count_z)
    quadrature = (
        gauss_weights[:, None, None] * weight_y[None, :, None] * weight_z[None, None, :] / 8.0
    )
    return spread[None] * jnp.asarray(quadrature, jnp.float32)


def pad_ends(field):
    return jnp.pad(field, ((0, 0), (0, 0), (0, 1), (0, 1)))


def gradient_of(own_nodes, right_layer, mats):
    return gradient(pad_ends(jnp.concatenate([own_nodes, right_layer[:, None]], axis=1)), mats)


def operate(own_nodes, right_layer, state, right_state, weighting, mats):
    terms = state_terms(gradient_of(state, right_state, mats))
    fluxes = tangent_flux(gradient_of(own_nodes, right_layer, mats), terms[0], terms[1], weighting)
    return divergence(fluxes, mats)[:, :, :-1, :-1]


def settle(image, field, rhs, keep, low_hat, high_hat, hat_y, hat_z):
    partial_value = rhs - keep * image[:, :4] - (1.0 - keep) * field
    coarse_terms = jnp.einsum("cjyz,vy,wz->cjvw", partial_value, hat_y, hat_z, precision=HIGHEST)
    onward = jnp.einsum("cjvw,j->cvw", coarse_terms, high_hat, precision=HIGHEST)
    arrived_layer, arrived_coarse = shifted((image[:, 4], onward), ("grp", "mem"), 1)
    fix_layer = -keep[0] * arrived_layer
    residual = partial_value.at[:, 0].add(fix_layer)
    own_coarse = (
        jnp.einsum("cjvw,j->cvw", coarse_terms, low_hat, precision=HIGHEST)
        + jnp.einsum("cyz,vy,wz->cvw", fix_layer, hat_y, hat_z, precision=HIGHEST)
        + arrived_coarse
    )
    return (residual, own_coarse)


def shards(state, direction, rhs, clamp, stiffness, coarse_owner, coarse_inverse):
    count_y = stiffness.shape[1]
    count_z = stiffness.shape[2]
    mats = operators(count_y, count_z)
    gll_points, gauss_weights, values, slopes = basis_tables()
    low_hat = jnp.asarray((1.0 - gll_points[:4]) / 2.0, jnp.float32)
    high_hat = jnp.asarray((1.0 + gll_points[:4]) / 2.0, jnp.float32)
    hat_y = jnp.asarray(restrictor(gll_points, count_y), jnp.float32)
    hat_z = jnp.asarray(restrictor(gll_points, count_z), jnp.float32)
    bottom = (jnp.arange(4 * count_z) == 0).astype(jnp.float32)
    keep = 1.0 - clamp.astype(jnp.float32)[:, :, None] * bottom[None, None, :]
    masked = keep * direction
    weighting = quad_weighting(stiffness[0], gauss_weights)
    right_direction, right_state, right_keep = shifted(
        (masked[:, 0], state[:, 0], keep[0, :, 0]), ("grp", "mem"), -1
    )
    image = operate(masked, right_direction, state, right_state, weighting, mats)
    first, restricted = settle(image, direction, rhs, keep, low_hat, high_hat, hat_y, hat_z)
    owner_slot = coarse_owner[0]
    flattened = restricted.reshape(3, count_y * count_z)
    outgoing = jnp.zeros_like(flattened).at[:, owner_slot].set(flattened)
    incoming = lax.all_to_all(outgoing, "grp", split_axis=1, concat_axis=1, tiled=True)
    blocks = coarse_inverse.shape[1]
    block_size = coarse_inverse.shape[2] // 3
    stacked = (
        incoming.reshape(3, blocks, block_size).transpose(1, 0, 2).reshape(blocks, 3 * block_size)
    )
    solved = jnp.einsum("kij,kj->ki", coarse_inverse[0], stacked, precision=HIGHEST)
    solved = (
        solved.reshape(blocks, 3, block_size).transpose(1, 0, 2).reshape(3, blocks * block_size)
    )
    returned = lax.all_to_all(solved, "grp", split_axis=1, concat_axis=1, tiled=True)
    correction = returned[:, owner_slot].reshape(3, count_y, count_z)
    right_correction = shifted(correction, ("grp", "mem"), -1)
    spread_own = jnp.einsum("cvw,vy,wz->cyz", correction, hat_y, hat_z, precision=HIGHEST)
    spread_right = jnp.einsum("cvw,vy,wz->cyz", right_correction, hat_y, hat_z, precision=HIGHEST)
    update = keep * (
        low_hat[None, :, None, None] * spread_own[:, None]
        + high_hat[None, :, None, None] * spread_right[:, None]
    )
    new_direction = direction + update
    keep_right = 1.0 - (1.0 - right_keep)[:, None] * bottom[None, :]
    right_new = right_direction + keep_right * spread_right
    image_next = operate(keep * new_direction, right_new, state, right_state, weighting, mats)
    residual, coarse_residual = settle(
        image_next, new_direction, rhs, keep, low_hat, high_hat, hat_y, hat_z
    )
    return (new_direction, residual, coarse_residual[:, None])


def solution(mesh):
    in_specs = (
        P(None, ("grp", "mem"), None, None),
        P(None, ("grp", "mem"), None, None),
        P(None, ("grp", "mem"), None, None),
        P(("grp", "mem"), None),
        P(("grp", "mem"), None, None),
        P(("grp", "mem"), None),
        P(("grp", "mem"), None, None, None),
    )
    out_specs = (
        P(None, ("grp", "mem"), None, None),
        P(None, ("grp", "mem"), None, None),
        P(None, ("grp", "mem"), None, None),
    )
    return jax.shard_map(shards, mesh=mesh, in_specs=in_specs, out_specs=out_specs, check_vma=False)
```

profile of v0, /device:TPU:8, one launch (start us, length us, event | category | flops | bytes accessed | tf_op | source)
XLA Modules:
  0.0 103.8 jit_solution(16769525344589389285)
XLA Ops:
  0.7 0.8 slice_bitcast_fusion.27
  1.5 3.7 %collective-permute-start.1 = (f32[3,16,128]{2,1,0:T(8,128)S(1)}, f32[3,16,128]{2,1,0:T(8,128)S(1)}, u32[]{:S(2)}, u32[]{:S(2)}) collective-permute-start(f32[3,16,128]{2,1,0:T(8,128)S(1)} %slice_bitcast_fusion.27), channel_id=1, source_target_pairs={{1,0},{2,1},{3,2},{4,3},{5,4},{6,5},{7,6},{8,7},{9,8},{10,9},{11,1... | collective-permute-start | bytes 73736 | tf_op jit(solution)/shard_map/ppermute | solution.py:15
  5.2 0.7 convert_element_type.21
  5.9 0.7 slice_reduce_fusion
  6.6 2.6 %collective-permute-start.5 = (f32[16]{0:T(128)}, f32[16]{0:T(128)}, u32[]{:S(2)}, u32[]{:S(2)}) collective-permute-start(f32[16]{0:T(128)} %slice_reduce_fusion), channel_id=1, source_target_pairs={{1,0},{2,1},{3,2},{4,3},{5,4},{6,5},{7,6},{8,7},{9,8},{10,9},{11,1... | collective-permute-start | bytes 200 | tf_op jit(solution)/shard_map/ppermute | solution.py:15
  9.2 1.9 %collective-permute-start = (f32[3,16,128]{2,1,0:T(8,128)S(1)}, f32[3,16,128]{2,1,0:T(8,128)S(1)}, u32[]{:S(2)}, u32[]{:S(2)}) collective-permute-start(f32[3,16,128]{2,1,0:T(8,128)S(1)} %slice_bitcast_fusion.26), channel_id=1, source_target_pairs={{1,0},{2,1},{3,2},{4,3},{5,4},{6,5},{7,6},{8,7},{9,8},{10,9},{11,1... | collective-permute-start | bytes 73736 | tf_op jit(solution)/shard_map/ppermute | solution.py:15
  26.9 0.8 convolution_bitcast_fusion.8
  31.2 3.2 %collective-permute-start.2 = (f32[3,16,128]{2,1,0:T(8,128)S(1)}, f32[3,16,128]{2,1,0:T(8,128)S(1)}, u32[]{:S(2)}, u32[]{:S(2)}) collective-permute-start(f32[3,16,128]{2,1,0:T(8,128)S(1)} %slice_bitcast_fusion.25), channel_id=1, source_target_pairs={{0,1},{1,2},{2,3},{3,4},{4,5},{5,6},{6,7},{7,8},{8,9},{9,10},{10,1... | collective-permute-start | bytes 73736 | tf_op jit(solution)/shard_map/ppermute | solution.py:15
  36.7 2.1 %collective-permute-start.3 = (f32[3,4,32]{2,1,0:T(4,128)S(1)}, f32[3,4,32]{2,1,0:T(4,128)S(1)}, u32[]{:S(2)}, u32[]{:S(2)}) collective-permute-start(f32[3,4,32]{2,1,0:T(4,128)S(1)} %bitcast.975), channel_id=1, source_target_pairs={{0,1},{1,2},{2,3},{3,4},{4,5},{5,6},{6,7},{7,8},{8,9},{9,10},{10,1... | collective-permute-start | bytes 4616 | tf_op jit(solution)/shard_map/ppermute | solution.py:15
  39.0 4.4 %collective-permute-done.3 = f32[3,4,32]{2,1,0:T(4,128)S(1)} collective-permute-done((f32[3,4,32]{2,1,0:T(4,128)S(1)}, f32[3,4,32]{2,1,0:T(4,128)S(1)}, u32[]{:S(2)}, u32[]{:S(2)}) %collective-permute-start.3) | collective-permute-done | bytes 1568 | tf_op jit(solution)/shard_map/ppermute | solution.py:15
  43.6 0.7 copy.339
  44.3 1.8 %scatter_custom_fusion = f32[3,128]{0,1:T(8,128)} fusion(s32[128]{0:T(128)S(1)} %fusion.131, f32[128,3]{1,0:T(8,128)} %bitcast.966, f32[]{:T(128)} %constant.82.clone.1), kind=kCustom, calls=%fused_computation.234 | custom fusion | bytes 2048 | tf_op jit(solution)/shard_map/scatter | solution.py:225
  46.1 1.6 %copy.263 = f32[3,8,16]{2,0,1:T(4,128)} copy(f32[3,8,16]{0,2,1:T(8,128)} %bitcast.963) | data formatting | bytes 3072 | tf_op jit(solution)/shard_map/all_to_all | solution.py:226
  47.6 5.3 %all-to-all-start = ((f32[3,8,16]{2,0,1:T(4,128)}), f32[3,8,16]{2,0,1:T(4,128)S(1)}, u32[]{:S(2)}, u32[]{:S(2)}) async-start(f32[3,8,16]{2,0,1:T(4,128)} %copy.263), calls=%async_computation | async-start | bytes 32768 | tf_op jit(solution)/shard_map/all_to_all | solution.py:226
  53.0 1.1 %broadcast_subtract_fusion.1 = f32[16]{0:T(128)} fusion(f32[16]{0:T(128)} %collective-permute-done.5), kind=kLoop, calls=%fused_computation.270 | loop fusion | flops 16 | bytes 128 | tf_op jit(solution)/shard_map/sub | solution.py:246
  54.1 3.9 %all-to-all-done = f32[3,8,16]{2,0,1:T(4,128)S(1)} async-done(((f32[3,8,16]{2,0,1:T(4,128)}), f32[3,8,16]{2,0,1:T(4,128)S(1)}, u32[]{:S(2)}, u32[]{:S(2)}) %all-to-all-start) | async-done | bytes 1568 | tf_op jit(solution)/shard_map/all_to_all | solution.py:226
  58.6 0.8 reshape.151
  60.7 4.8 %all-to-all-start.1 = ((f32[3,8,16]{2,0,1:T(4,128)}), f32[3,8,16]{2,0,1:T(4,128)S(1)}, u32[]{:S(2)}, u32[]{:S(2)}) async-start(f32[3,8,16]{2,0,1:T(4,128)} %copy.267), calls=%async_computation.1 | async-start | bytes 32768 | tf_op jit(solution)/shard_map/all_to_all | solution.py:236
  65.5 1.3 %multiply_subtract_fusion.1 = f32[16,128]{1,0:T(8,128)} fusion(f32[128]{0:T(128)} %copy-done.30, f32[16]{0:T(128)} %broadcast_subtract_fusion.1), kind=kLoop, calls=%fused_computation.264 | loop fusion | flops 4096 | bytes 8768 | tf_op jit(solution)/shard_map/sub | solution.py:246
  66.8 3.7 %all-to-all-done.1 = f32[3,8,16]{2,0,1:T(4,128)S(1)} async-done(((f32[3,8,16]{2,0,1:T(4,128)}), f32[3,8,16]{2,0,1:T(4,128)S(1)}, u32[]{:S(2)}, u32[]{:S(2)}) %all-to-all-start.1) | async-done | bytes 1568 | tf_op jit(solution)/shard_map/all_to_all | solution.py:236
  70.5 0.8 copy.268
  71.3 2.2 %gather_fusion = f32[128,3]{1,0:T(8,128)} fusion(f32[3,128]{0,1:T(8,128)} %bitcast.964, s32[1024]{0:T(1024)} %pad_clamp_fusion), kind=kCustom, calls=%fused_computation | custom fusion | bytes 3584 | tf_op jit(solution)/shard_map/gather | solution.py:237
  73.5 0.9 copy.340
  74.6 1.9 %collective-permute-start.4 = (f32[3,4,32]{2,1,0:T(4,128)S(1)}, f32[3,4,32]{2,1,0:T(4,128)S(1)}, u32[]{:S(2)}, u32[]{:S(2)}) collective-permute-start(f32[3,4,32]{2,1,0:T(4,128)S(1)} %copy.340), channel_id=1, source_target_pairs={{1,0},{2,1},{3,2},{4,3},{5,4},{6,5},{7,6},{8,7},{9,8},{10,9},{11,1... | collective-permute-start | bytes 4616 | tf_op jit(solution)/shard_map/ppermute | solution.py:15
  76.7 1.1 %collective-permute-done.4 = f32[3,4,32]{2,1,0:T(4,128)S(1)} collective-permute-done((f32[3,4,32]{2,1,0:T(4,128)S(1)}, f32[3,4,32]{2,1,0:T(4,128)S(1)}, u32[]{:S(2)}, u32[]{:S(2)}) %collective-permute-start.4) | collective-permute-done | bytes 1568 | tf_op jit(solution)/shard_map/ppermute | solution.py:15
  91.4 0.7 copy-done.22
  93.6 1.9 %collective-permute-start.6 = (f32[3,16,128]{2,1,0:T(8,128)S(1)}, f32[3,16,128]{2,1,0:T(8,128)S(1)}, u32[]{:S(2)}, u32[]{:S(2)}) collective-permute-start(f32[3,16,128]{2,1,0:T(8,128)S(1)} %slice_bitcast_fusion.24), channel_id=1, source_target_pairs={{0,1},{1,2},{2,3},{3,4},{4,5},{5,6},{6,7},{7,8},{8,9},{9,10},{10,1... | collective-permute-start | bytes 73736 | tf_op jit(solution)/shard_map/ppermute | solution.py:15
  96.3 1.9 %collective-permute-start.7 = (f32[3,4,32]{2,1,0:T(4,128)S(1)}, f32[3,4,32]{2,1,0:T(4,128)S(1)}, u32[]{:S(2)}, u32[]{:S(2)}) collective-permute-start(f32[3,4,32]{2,1,0:T(4,128)S(1)} %bitcast.974), channel_id=1, source_target_pairs={{0,1},{1,2},{2,3},{3,4},{4,5},{5,6},{6,7},{7,8},{8,9},{9,10},{10,1... | collective-permute-start | bytes 4616 | tf_op jit(solution)/shard_map/ppermute | solution.py:15
  98.3 2.3 %collective-permute-done.6 = f32[3,16,128]{2,1,0:T(8,128)S(1)} collective-permute-done((f32[3,16,128]{2,1,0:T(8,128)S(1)}, f32[3,16,128]{2,1,0:T(8,128)S(1)}, u32[]{:S(2)}, u32[]{:S(2)}) %collective-permute-start.6) | collective-permute-done | bytes 24608 | tf_op jit(solution)/shard_map/ppermute | solution.py:15
  100.7 0.7 copy.291
  101.3 1.8 %collective-permute-done.7 = f32[3,4,32]{2,1,0:T(4,128)S(1)} collective-permute-done((f32[3,4,32]{2,1,0:T(4,128)S(1)}, f32[3,4,32]{2,1,0:T(4,128)S(1)}, u32[]{:S(2)}, u32[]{:S(2)}) %collective-permute-start.7) | collective-permute-done | bytes 1568 | tf_op jit(solution)/shard_map/ppermute | solution.py:15
  103.1 0.8 fusion.4
  (174 shorter events, 39.6 us)
Async XLA Ops:
  0.6 58.8 %copy-start = (f32[1,2,192,192]{3,2,1,0:T(8,128)S(1)}, f32[1,2,192,192]{3,2,1,0:T(8,128)}, u32[]{:S(2)}) copy-start(f32[1,2,192,192]{3,2,1,0:T(8,128)} %param.26) | copy-start | bytes 884740
  0.6 8.5 %copy-start.3 = (f32[3,4,16,128]{3,2,1,0:T(8,128)S(1)}, f32[3,4,16,128]{3,2,1,0:T(8,128)}, u32[]{:S(2)}) copy-start(f32[3,4,16,128]{3,2,1,0:T(8,128)} %param.21) | copy-start | bytes 294916
  1.5 12.8 %collective-permute-start.1 = (f32[3,16,128]{2,1,0:T(8,128)S(1)}, f32[3,16,128]{2,1,0:T(8,128)S(1)}, u32[]{:S(2)}, u32[]{:S(2)}) collective-permute-start(f32[3,16,128]{2,1,0:T(8,128)S(1)} %slice_bitcast_fusion.27), channel_id=1, source_target_pairs={{1,0},{2,1},{3,2},{4,3},{5,4},{6,5},{7,6},{8,7},{9,8},{10,9},{11,1... | collective-permute-start | bytes 73736 | tf_op jit(solution)/shard_map/ppermute | solution.py:15
  6.6 46.4 %collective-permute-start.5 = (f32[16]{0:T(128)}, f32[16]{0:T(128)}, u32[]{:S(2)}, u32[]{:S(2)}) collective-permute-start(f32[16]{0:T(128)} %slice_reduce_fusion), channel_id=1, source_target_pairs={{1,0},{2,1},{3,2},{4,3},{5,4},{6,5},{7,6},{8,7},{9,8},{10,9},{11,1... | collective-permute-start | bytes 200 | tf_op jit(solution)/shard_map/ppermute | solution.py:15
  9.2 2.0 %copy-start.34 = (s32[1,128]{1,0:T(1,128)S(1)}, s32[1,128]{1,0:T(1,128)}, u32[]{:S(2)}) copy-start(s32[1,128]{1,0:T(1,128)} %param.25) | copy-start | bytes 1540
  9.2 3.4 %collective-permute-start = (f32[3,16,128]{2,1,0:T(8,128)S(1)}, f32[3,16,128]{2,1,0:T(8,128)S(1)}, u32[]{:S(2)}, u32[]{:S(2)}) collective-permute-start(f32[3,16,128]{2,1,0:T(8,128)S(1)} %slice_bitcast_fusion.26), channel_id=1, source_target_pairs={{1,0},{2,1},{3,2},{4,3},{5,4},{6,5},{7,6},{8,7},{9,8},{10,9},{11,1... | collective-permute-start | bytes 73736 | tf_op jit(solution)/shard_map/ppermute | solution.py:15
  12.0 0.9 copy-start.11
  12.9 0.9 copy-start.13
  13.8 0.9 copy-start.25
  15.1 0.7 copy-start.9
  22.3 0.9 copy-start.1
  28.8 0.9 copy-start.5
  29.7 0.9 copy-start.4
  30.6 3.8 %copy-start.7 = (f32[3,4,16,128]{3,2,1,0:T(8,128)S(1)}, f32[3,4,16,128]{3,2,1,0:T(8,128)}, u32[]{:S(2)}) copy-start(f32[3,4,16,128]{3,2,1,0:T(8,128)} %param.22) | copy-start | bytes 294916
  31.1 3.3 %copy-start.21 = (f32[4,16,1,1]{1,0,3,2:T(4,128)S(1)}, f32[4,16,1,1]{1,0,3,2:T(4,128)}, u32[]{:S(2)}) copy-start(f32[4,16,1,1]{1,0,3,2:T(4,128)} %constant.115) | copy-start | bytes 772
  31.1 7.7 %copy-start.23 = (f32[4,16,1]{1,0,2:T(4,128)S(1)}, f32[4,16,1]{1,0,2:T(4,128)}, u32[]{:S(2)}) copy-start(f32[4,16,1]{1,0,2:T(4,128)} %constant.126) | copy-start | bytes 772
  31.2 7.6 %collective-permute-start.2 = (f32[3,16,128]{2,1,0:T(8,128)S(1)}, f32[3,16,128]{2,1,0:T(8,128)S(1)}, u32[]{:S(2)}, u32[]{:S(2)}) collective-permute-start(f32[3,16,128]{2,1,0:T(8,128)S(1)} %slice_bitcast_fusion.25), channel_id=1, source_target_pairs={{0,1},{1,2},{2,3},{3,4},{4,5},{5,6},{6,7},{7,8},{8,9},{9,10},{10,1... | collective-permute-start | bytes 73736 | tf_op jit(solution)/shard_map/ppermute | solution.py:15
  34.4 0.7 copy-start.16
  36.6 6.8 %copy-start.10 = (f32[32,128,1]{1,0,2:T(8,128)S(1)}, f32[32,128,1]{1,0,2:T(8,128)}, u32[]{:S(2)}) copy-start(f32[32,128,1]{1,0,2:T(8,128)} %constant.114) | copy-start | bytes 49156
  36.7 6.7 %collective-permute-start.3 = (f32[3,4,32]{2,1,0:T(4,128)S(1)}, f32[3,4,32]{2,1,0:T(4,128)S(1)}, u32[]{:S(2)}, u32[]{:S(2)}) collective-permute-start(f32[3,4,32]{2,1,0:T(4,128)S(1)} %bitcast.975), channel_id=1, source_target_pairs={{0,1},{1,2},{2,3},{3,4},{4,5},{5,6},{6,7},{7,8},{8,9},{9,10},{10,1... | collective-permute-start | bytes 4616 | tf_op jit(solution)/shard_map/ppermute | solution.py:15
  47.6 10.3 %all-to-all-start = ((f32[3,8,16]{2,0,1:T(4,128)}), f32[3,8,16]{2,0,1:T(4,128)S(1)}, u32[]{:S(2)}, u32[]{:S(2)}) async-start(f32[3,8,16]{2,0,1:T(4,128)} %copy.263), calls=%async_computation | async-start | bytes 32768 | tf_op jit(solution)/shard_map/all_to_all | solution.py:226
  60.7 9.9 %all-to-all-start.1 = ((f32[3,8,16]{2,0,1:T(4,128)}), f32[3,8,16]{2,0,1:T(4,128)S(1)}, u32[]{:S(2)}, u32[]{:S(2)}) async-start(f32[3,8,16]{2,0,1:T(4,128)} %copy.267), calls=%async_computation.1 | async-start | bytes 32768 | tf_op jit(solution)/shard_map/all_to_all | solution.py:236
  74.4 2.1 %copy-start.24 = (f32[4,16,1]{1,0,2:T(4,128)S(1)}, f32[4,16,1]{1,0,2:T(4,128)}, u32[]{:S(2)}) copy-start(f32[4,16,1]{1,0,2:T(4,128)} %constant.126) | copy-start | bytes 772
  74.6 3.3 %collective-permute-start.4 = (f32[3,4,32]{2,1,0:T(4,128)S(1)}, f32[3,4,32]{2,1,0:T(4,128)S(1)}, u32[]{:S(2)}, u32[]{:S(2)}) collective-permute-start(f32[3,4,32]{2,1,0:T(4,128)S(1)} %copy.340), channel_id=1, source_target_pairs={{1,0},{2,1},{3,2},{4,3},{5,4},{6,5},{7,6},{8,7},{9,8},{10,9},{11,1... | collective-permute-start | bytes 4616 | tf_op jit(solution)/shard_map/ppermute | solution.py:15
  78.7 0.8 copy-start.20
  78.7 0.9 copy-start.12
  79.6 0.9 copy-start.14
  90.4 0.9 copy-start.8
  92.0 0.7 copy-start.17
  93.4 2.1 %copy-start.27 = (f32[4,1,1,1]{0,1,3,2:T(1,128)S(1)}, f32[4,1,1,1]{0,1,3,2:T(1,128)}, u32[]{:S(2)}) copy-start(f32[4,1,1,1]{0,1,3,2:T(1,128)} %constant.125) | copy-start | bytes 52
  93.6 6.9 %collective-permute-start.6 = (f32[3,16,128]{2,1,0:T(8,128)S(1)}, f32[3,16,128]{2,1,0:T(8,128)S(1)}, u32[]{:S(2)}, u32[]{:S(2)}) collective-permute-start(f32[3,16,128]{2,1,0:T(8,128)S(1)} %slice_bitcast_fusion.24), channel_id=1, source_target_pairs={{0,1},{1,2},{2,3},{3,4},{4,5},{5,6},{6,7},{7,8},{8,9},{9,10},{10,1... | collective-permute-start | bytes 73736 | tf_op jit(solution)/shard_map/ppermute | solution.py:15
  96.3 6.7 %collective-permute-start.7 = (f32[3,4,32]{2,1,0:T(4,128)S(1)}, f32[3,4,32]{2,1,0:T(4,128)S(1)}, u32[]{:S(2)}, u32[]{:S(2)}) collective-permute-start(f32[3,4,32]{2,1,0:T(4,128)S(1)} %bitcast.974), channel_id=1, source_target_pairs={{0,1},{1,2},{2,3},{3,4},{4,5},{5,6},{6,7},{7,8},{8,9},{9,10},{10,1... | collective-permute-start | bytes 4616 | tf_op jit(solution)/shard_map/ppermute | solution.py:15
  (13 other events, 8.8 us)
where the time goes:
time: 105 us; the launch traced here: 104 us
  starting transfers between devices  29.4 us (28%)
  matrix products  24.7 us (24%)
  local copies, waits for them, and re-layouts  21.6 us (21%)
  waiting for transfers between devices  17.8 us (17%)
  other arithmetic  8.9 us (8%)
  between operations  1.46 us (1%)
    ppermute x8, starting transfers between devices, shifted(): return lax.ppermute(block, axis, route)  19.3 us
    ppermute x8, waiting for transfers between devices, shifted(): return lax.ppermute(block, axis, route)  10.1 us
    unnamed x72, local copies, waits for them, and re-layouts  9.68 us
    all_to_all x1, starting transfers between devices, shards(): lax.all_to_all(outgoing, 'grp', split_axis=1, concat_axis=1, tiled=True)  5.32 us
    another operation x18, other arithmetic, tangent_flux(): fluxes.append(jnp.stack(rows_of))  4.95 us
    all_to_all x1, starting transfers between devices, shards(): lax.all_to_all(solved, 'grp', split_axis=1, concat_axis=1, tiled=True)  4.79 us
    all_to_all x1, waiting for transfers between devices, shards(): lax.all_to_all(outgoing, 'grp', split_axis=1, concat_axis=1, tiled=True)  3.92 us
    all_to_all x1, waiting for transfers between devices, shards(): lax.all_to_all(solved, 'grp', split_axis=1, concat_axis=1, tiled=True)  3.74 us
  transfers between devices with their start and end apart: 10, of which 7 were waited for; matrix products, arithmetic and copies ran while one was open for 26% of the time, Pallas kernels for 0%

commit v1 on v0

v1 whole, which is shorter than its diff:
```python
import functools

import jax
import jax.numpy as jnp
import ml_dtypes
import numpy as np
from jax import lax
from jax.experimental import pallas as pl
from jax.experimental.pallas import tpu as pltpu
from jax.sharding import PartitionSpec as P

LAME_FIRST = 1.2
LAME_SHEAR = 0.8
HIGHEST = lax.Precision.HIGHEST
MESH = pl.DeviceIdType.MESH
F32 = jnp.float32
BF16 = jnp.bfloat16
NQ = 112


def gauss_rule():
    inner = np.sqrt(5.0 - 2.0 * np.sqrt(10.0 / 7.0)) / 3.0
    outer = np.sqrt(5.0 + 2.0 * np.sqrt(10.0 / 7.0)) / 3.0
    inner_weight = (322.0 + 13.0 * np.sqrt(70.0)) / 900.0
    outer_weight = (322.0 - 13.0 * np.sqrt(70.0)) / 900.0
    points = np.array([-outer, -inner, 0.0, inner, outer])
    weights = np.array([outer_weight, inner_weight, 128.0 / 225.0, inner_weight, outer_weight])
    return (points, weights)


def basis_tables():
    gll_points = np.array([-1.0, -np.sqrt(3.0 / 7.0), 0.0, np.sqrt(3.0 / 7.0), 1.0])
    gauss_points, gauss_weights = gauss_rule()
    values = np.zeros((5, 5))
    slopes = np.zeros((5, 5))
    for j in range(5):
        others = [gll_points[k] for k in range(5) if k != j]
        denominator = np.prod([gll_points[j] - o for o in others])
        for q in range(5):
            t = gauss_points[q]
            values[q, j] = np.prod([t - o for o in others]) / denominator
            total = 0.0
            for i in range(4):
                total += np.prod([t - others[k] for k in range(4) if k != i])
            slopes[q, j] = 2.0 * total / denominator
    return (gll_points, gauss_weights, values, slopes)


def banded(table, count):
    banded_matrix = np.zeros((5 * count, 4 * count + 1))
    for e in range(count):
        banded_matrix[5 * e : 5 * e + 5, 4 * e : 4 * e + 5] = table
    return banded_matrix[:, :-1]


def restrictor(gll_points, count):
    result = np.zeros((count, 4 * count))
    for e in range(count):
        for j in range(4):
            result[e, 4 * e + j] += (1.0 - gll_points[j]) / 2.0
            if e + 1 < count:
                result[e + 1, 4 * e + j] += (1.0 + gll_points[j]) / 2.0
    return result


def halves(table):
    high = table.astype(ml_dtypes.bfloat16)
    low = (table - high.astype(np.float64)).astype(ml_dtypes.bfloat16)
    return high, low


def padded(table, axis, multiple):
    widths = [(0, 0), (0, 0)]
    widths[axis] = (0, -table.shape[axis] % multiple)
    return np.pad(table, widths)


def left_table(table):
    high, low = halves(table)
    return padded(np.concatenate([high, high, low], axis=1), 1, 128)


def right_table(table):
    high, low = halves(table)
    return np.concatenate([high, high, low], axis=0)


def constant_tables(count_y, count_z):
    gll_points, weights, values, slopes = basis_tables()
    by, dy = banded(values, count_y), banded(slopes, count_y)
    bz, dz = banded(values, count_z), banded(slopes, count_z)
    pads = lambda t: np.pad(t, ((0, NQ - t.shape[0]), (0, 0)))
    cross = np.concatenate(
        [pads(np.kron(slopes, by)), pads(np.kron(values, dy)), pads(np.kron(values, by))]
    )
    bz, dz = padded(bz, 0, 256), padded(dz, 0, 256)
    low_hat = np.append((1.0 - gll_points[:4]) / 2.0, 0.0)
    high_hat = np.append((1.0 + gll_points[:4]) / 2.0, 1.0)
    hat_y = restrictor(gll_points, count_y)
    hat_z = restrictor(gll_points, count_z)
    hats = np.zeros((16, 20 * count_y))
    hats[:count_y] = np.kron(low_hat[None], hat_y)
    hats[8 : 8 + count_y] = np.kron(high_hat[None], hat_y)
    tiled = np.tile(hat_z, (count_y, 1))
    spread_y = np.zeros((NQ, count_y))
    spread_y[:100] = np.kron(weights[:, None], np.kron(np.eye(count_y), weights[:, None])) / 8.0
    spread_z = padded(np.kron(np.eye(count_z), weights[None]), 1, 256)
    return (
        left_table(cross),
        right_table(bz.T),
        right_table(dz.T),
        np.concatenate(halves(bz), axis=1),
        np.concatenate(halves(dz), axis=1),
        left_table(cross.T),
        left_table(hats),
        right_table(tiled.T),
        right_table(tiled),
        left_table(hats.T),
        spread_y.astype(np.float32),
        spread_z.astype(np.float32),
    )


def split(x):
    high = x.astype(BF16)
    return high, (x - high.astype(F32)).astype(BF16)


def dot(a, b):
    return lax.dot_general(a, b, (((1,), (0,)), ((), ())), preferred_element_type=F32)


def dot_nt(a, b):
    return lax.dot_general(a, b, (((1,), (1,)), ((), ())), preferred_element_type=F32)


def times_right(x, table):
    high, low = split(x)
    return dot(jnp.concatenate([high, low, high], axis=1), table)


def times_left(table, x):
    high, low = split(x)
    parts = [high, low, high]
    rest = table.shape[1] - 3 * x.shape[0]
    if rest:
        parts.append(jnp.zeros((rest, x.shape[1]), BF16))
    return dot(table, jnp.concatenate(parts, axis=0))


def stacked_exact(x, one_hot, product):
    rows = x.shape[0]
    high, low = split(x)
    both = product(jnp.concatenate([high, low], axis=0), one_hot)
    return both[:rows] + both[rows:]


def iota(shape, axis):
    return lax.broadcasted_iota(jnp.int32, shape, axis)


def each(low, high, act):
    if high - low <= 8:
        for i in range(low, high):
            act(i)
    else:

        def step(i, carry):
            act(i)
            return carry

        lax.fori_loop(low, high, step, 0)


def kernel(
    groups,
    members,
    state_ref,
    direction_ref,
    rhs_ref,
    clamp_ref,
    stiff_ref,
    owner_ref,
    inverse_ref,
    cross_ref,
    bz_ref,
    dz_ref,
    bzt_ref,
    dzt_ref,
    crosst_ref,
    hats_ref,
    hatz_ref,
    hatzp_ref,
    hatst_ref,
    spready_ref,
    spreadz_ref,
    new_ref,
    residual_ref,
    coarse_ref,
    halo_tx,
    halo_state,
    halo_rx,
    sums_tx,
    sums_rx,
    solved_tx,
    solved_rx,
    last_tx,
    last_rx,
    inv_high,
    inv_low,
    weight,
    gsb,
    gsz,
    gvb,
    gvz,
    deform_s,
    stress_s,
    fbh,
    fbl,
    fzh,
    fzl,
    halo_send,
    halo_recv,
    sums_send,
    sums_recv,
    solved_send,
    solved_recv,
    last_send,
    last_recv,
):
    count_y, count_z = stiff_ref.shape[1:]
    ny = 4 * count_y
    vertices = count_y * count_z
    blocks = inverse_ref.shape[1]
    size = inverse_ref.shape[2]
    block = size // 3
    message = vertices // groups
    per_block = groups // blocks
    g = lax.axis_index("grp")
    m = lax.axis_index("mem")
    m_right = lax.rem(m + 1, members)
    m_left = lax.rem(m + members - 1, members)
    at_end = m == members - 1
    at_start = m == 0
    g_right = lax.rem(g + at_end.astype(jnp.int32), groups)
    g_left = lax.rem(g + groups - at_start.astype(jnp.int32), groups)
    is_last = (g * members + m) == groups * members - 1
    is_first = (g * members + m) == 0

    barrier = pltpu.get_barrier_semaphore()

    def greet(p, member):
        pl.semaphore_signal(barrier, inc=1, device_id=(p, member), device_id_type=MESH)

    sums_rx[...] = jnp.zeros_like(sums_rx)
    greet(g_left, m_left)
    each(1, groups, lambda d: greet(lax.rem(g_left + d, groups), m_left))
    each(0, groups, lambda d: greet(lax.rem(g_right + d, groups), m_right))
    each(1, groups, lambda d: greet(lax.rem(g + d, groups), m))

    eye = iota((ny, ny), 0) == iota((ny, ny), 1)
    clamp_rows = []
    for x in range(4):
        row = jnp.broadcast_to(clamp_ref[x : x + 1, :].astype(F32), (ny, ny))
        clamp_rows.append(jnp.sum(jnp.where(eye, row, 0.0), axis=1, keepdims=True))
    clamped = jnp.concatenate(clamp_rows, axis=0)
    lanes = 4 * count_z
    keep = jnp.where(iota((4 * ny, lanes), 1) == 0, 1.0 - clamped, 1.0)
    for c in range(3):
        halo_tx[c * ny : (c + 1) * ny, :] = keep[:ny] * direction_ref[c, 0]
    halo_tx[3 * ny : 4 * ny, :] = keep[:ny]
    halo_tx[4 * ny : 4 * ny + 8, :] = jnp.broadcast_to(owner_ref[...].astype(F32), (8, vertices))
    pl.semaphore_wait(barrier, 3 * groups - 1)

    left = (g_left, m_left)
    right = (g_right, m_right)

    def remote(src, dst, send, recv, device):
        return pltpu.make_async_remote_copy(
            src_ref=src, dst_ref=dst, send_sem=send, recv_sem=recv, device_id=device, device_id_type=MESH
        )

    copy_state = remote(state_ref.at[:, 0], halo_state, halo_send.at[0], halo_recv.at[0], left)
    copy_state.start()
    copy_halo = remote(halo_tx, halo_rx, halo_send.at[1], halo_recv.at[1], left)
    copy_halo.start()

    inv_high[...] = jnp.zeros_like(inv_high)
    inv_low[...] = jnp.zeros_like(inv_low)
    for b in range(blocks):
        high, low = split(inverse_ref[0, b])
        inv_high[b, :size, :size] = high
        inv_low[b, :size, :size] = low
    along_y = jnp.zeros((NQ, count_z), F32)
    for k in range(count_y):
        along_y = along_y + spready_ref[:, k : k + 1] * stiff_ref[0, k : k + 1, :]
    weight[...] = jnp.dot(along_y, spreadz_ref[...], precision=HIGHEST, preferred_element_type=F32)
    own_hot = (owner_ref[...] == iota((vertices, vertices), 0)).astype(F32).astype(BF16)

    def gradients(field, to_b, to_z):
        parts = times_left(cross_ref[...], field)
        plain = jnp.concatenate([parts[: 2 * NQ, c * lanes : (c + 1) * lanes] for c in range(3)], axis=0)
        sloped = jnp.concatenate([parts[2 * NQ :, c * lanes : (c + 1) * lanes] for c in range(3)], axis=0)
        to_b[...] = times_right(plain, bz_ref[...])
        to_z[...] = times_right(sloped, dz_ref[...])

    def load_change(from_b, from_z, r, s):
        change = []
        for c in range(3):
            change.append(
                [
                    from_b[pl.ds(pl.multiple_of(c * 2 * NQ + r, 16), 16), s],
                    from_b[pl.ds(pl.multiple_of(c * 2 * NQ + NQ + r, 16), 16), s],
                    from_z[pl.ds(pl.multiple_of(c * NQ + r, 16), 16), s],
                ]
            )
        return change

    pairs = [(0, 0), (1, 1), (2, 2), (0, 1), (0, 2), (1, 2)]

    def fluxes(first):
        def body(i, carry):
            r = pl.multiple_of(i * 16, 16)
            for half in range(2):
                s = pl.ds(half * 128, 128)
                w = weight[pl.ds(r, 16), s]
                if first:
                    grad = load_change(gsb, gsz, r, s)
                    deform = [[grad[c][a] + 1.0 if c == a else grad[c][a] for a in range(3)] for c in range(3)]
                    cg = [sum(deform[k][a] * deform[k][b] for k in range(3)) for a, b in pairs]
                    trace = (0.5 * LAME_FIRST) * (cg[0] + cg[1] + cg[2]) - 1.5 * LAME_FIRST
                    stress = [LAME_SHEAR * t for t in cg]
                    stress = [w * (t - LAME_SHEAR + trace) for t in stress[:3]] + [w * t for t in stress[3:]]
                    for c in range(3):
                        for a in range(3):
                            deform_s[3 * c + a, pl.ds(r, 16), s] = deform[c][a]
                    for k in range(6):
                        stress_s[k, pl.ds(r, 16), s] = stress[k]
                else:
                    deform = [[deform_s[3 * c + a, pl.ds(r, 16), s] for a in range(3)] for c in range(3)]
                    stress = [stress_s[k, pl.ds(r, 16), s] for k in range(6)]
                change = load_change(gvb, gvz, r, s)
                diagonal = [sum(deform[k][a] * change[k][a] for k in range(3)) for a in range(3)]
                trace = LAME_FIRST * (diagonal[0] + diagonal[1] + diagonal[2])
                moved = [w * (2.0 * LAME_SHEAR * t + trace) for t in diagonal]
                shear = LAME_SHEAR * w
                for a, b in pairs[3:]:
                    moved.append(
                        shear * sum(deform[k][a] * change[k][b] + deform[k][b] * change[k][a] for k in range(3))
                    )
                at = [[0, 3, 4], [3, 1, 5], [4, 5, 2]]
                for c in range(3):
                    for a in range(3):
                        entry = sum(change[c][b] * stress[at[b][a]] + deform[c][b] * moved[at[b][a]] for b in range(3))
                        high, low = split(entry)
                        if a < 2:
                            place = pl.ds(pl.multiple_of(c * 2 * NQ + a * NQ + r, 16), 16)
                            fbh[place, s] = high
                            fbl[place, s] = low
                        else:
                            place = pl.ds(pl.multiple_of(c * NQ + r, 16), 16)
                            fzh[place, s] = high
                            fzl[place, s] = low
            return carry

        lax.fori_loop(0, NQ // 16, body, 0)

    def divergence():
        both_b = dot(fbh[...], bzt_ref[...])
        both_z = dot(fzh[...], dzt_ref[...])
        side_b = both_b[:, :lanes] + both_b[:, lanes:] + dot(fbl[...], bzt_ref[:, :lanes])
        side_z = both_z[:, :lanes] + both_z[:, lanes:] + dot(fzl[...], dzt_ref[:, :lanes])
        columns = [
            jnp.concatenate([side_b[c * 2 * NQ : (c + 1) * 2 * NQ], side_z[c * NQ : (c + 1) * NQ]], axis=0)
            for c in range(3)
        ]
        return times_left(crosst_ref[...], jnp.concatenate(columns, axis=1))

    vertex_of_row = lax.rem(iota((48, vertices), 0), 8)
    vertex_mask = vertex_of_row == iota((48, vertices), 1) // count_z

    def restrict(field):
        rows = times_left(hats_ref[...], field)
        rows = jnp.concatenate([rows[:, c * lanes : (c + 1) * lanes] for c in range(3)], axis=0)
        rows = jnp.where(vertex_mask, times_right(rows, hatz_ref[...]), 0.0)
        rows = [jnp.sum(rows[8 * i : 8 * i + 8], axis=0, keepdims=True) for i in range(6)]
        fill = jnp.zeros((5, vertices), F32)
        return (
            jnp.concatenate([rows[0], rows[2], rows[4], fill], axis=0),
            jnp.concatenate([rows[1], rows[3], rows[5], fill], axis=0),
        )

    def widened(own, beyond):
        return jnp.concatenate([jnp.concatenate([own[c], beyond[c]], axis=0) for c in range(3)], axis=1)

    own_state = [state_ref[c].reshape(4 * ny, lanes) for c in range(3)]
    own_direction = [direction_ref[c].reshape(4 * ny, lanes) for c in range(3)]
    own_rhs = [rhs_ref[c].reshape(4 * ny, lanes) for c in range(3)]

    copy_state.wait_recv()
    beyond_state = [jnp.where(is_last, 0.0, halo_state[c]) for c in range(3)]
    gradients(widened(own_state, beyond_state), gsb, gsz)
    copy_halo.wait_recv()
    beyond_direction = [jnp.where(is_last, 0.0, halo_rx[c * ny : (c + 1) * ny, :]) for c in range(3)]
    keep_right = halo_rx[3 * ny : 4 * ny, :]
    owner_right = halo_rx[4 * ny : 4 * ny + 1, :].astype(jnp.int32)
    right_hot = (owner_right == iota((vertices, vertices), 0)).astype(F32).astype(BF16)
    gradients(widened([keep * own_direction[c] for c in range(3)], beyond_direction), gvb, gvz)
    fluxes(True)
    image = divergence()

    def settle(image, field):
        own, beyond = [], []
        for c in range(3):
            part = image[:, c * lanes : (c + 1) * lanes]
            own.append(own_rhs[c] - keep * part[: 4 * ny] - (1.0 - keep) * field[c])
            beyond.append(-keep_right * part[4 * ny :])
        return own, beyond

    own_first, beyond_first = settle(image, own_direction)
    low_sums, high_sums = restrict(widened(own_first, beyond_first))
    high_sums = jnp.where(is_last, 0.0, high_sums)
    sums_tx[0] = stacked_exact(low_sums, own_hot, dot_nt)
    sums_tx[1] = stacked_exact(high_sums, right_hot, dot_nt)

    def send_own(d):
        p = lax.rem(g + d, groups)
        remote(
            sums_tx.at[0, pl.ds(0, 4)], sums_rx.at[g, pl.ds(0, 4)], sums_send.at[d], sums_recv.at[g], (p, m)
        ).start()

    def send_next(d):
        p = lax.rem(g_right + d, groups)
        remote(
            sums_tx.at[1, pl.ds(0, 4)],
            sums_rx.at[groups + g_right, pl.ds(0, 4)],
            sums_send.at[groups + d],
            sums_recv.at[groups + g_right],
            (p, m_right),
        ).start()

    each(0, groups, send_next)
    each(1, groups, send_own)
    sums_rx[g] = sums_tx[0]

    def got_own(d):
        p = lax.rem(g + d, groups)
        remote(
            sums_tx.at[0, pl.ds(0, 4)], sums_rx.at[p, pl.ds(0, 4)], sums_send.at[d], sums_recv.at[p], (p, m)
        ).wait()

    def got_next(p):
        remote(
            sums_tx.at[1, pl.ds(0, 4)],
            sums_rx.at[groups + p, pl.ds(0, 4)],
            sums_send.at[groups + p],
            sums_recv.at[groups + p],
            right,
        ).wait()

    each(1, groups, got_own)
    each(0, groups, got_next)

    wide = inv_high.shape[2]
    received = sums_rx[:groups] + sums_rx[groups:]
    received = received.reshape(groups * 8, vertices)
    pick = (
        iota((vertices, wide), 0) == g * message + lax.rem(iota((vertices, wide), 1), message)
    ).astype(F32).astype(BF16)
    placed = stacked_exact(received, pick, dot)
    shape = (groups * 8, wide)
    row, lane = iota(shape, 0), iota(shape, 1)
    placed = jnp.where(
        (lane // block == lax.rem(row, 8))
        & (lax.rem(lane, block) // message == lax.rem(row // 8, per_block))
        & (lane < size),
        placed,
        0.0,
    )
    vectors = [
        jnp.sum(placed[b * per_block * 8 : (b + 1) * per_block * 8], axis=0, keepdims=True) for b in range(blocks)
    ]
    for b in range(blocks):
        high, low = split(jnp.broadcast_to(vectors[b], (8, wide)))
        both = dot_nt(jnp.concatenate([high, low], axis=0), inv_high[b])
        solved_tx[b] = (both[:1] + both[8:9]) + dot_nt(jnp.concatenate([high, high], axis=0), inv_low[b])[:1]

    def return_own(d):
        p = lax.rem(g + d, groups)
        remote(
            solved_tx.at[p // per_block], solved_rx.at[g], solved_send.at[d], solved_recv.at[g], (p, m)
        ).start()

    def return_left(d):
        p = lax.rem(g + d, groups)
        before = lax.rem(p + groups - at_start.astype(jnp.int32), groups)
        remote(
            solved_tx.at[p // per_block],
            solved_rx.at[groups + g],
            solved_send.at[groups + d],
            solved_recv.at[groups + g],
            (before, m_left),
        ).start()

    each(0, groups, return_left)
    each(1, groups, return_own)
    solved_rx[g] = solved_tx[g // per_block]

    def back_own(d):
        p = lax.rem(g + d, groups)
        remote(solved_tx.at[0], solved_rx.at[p], solved_send.at[d], solved_recv.at[p], (p, m)).wait()

    def back_next(p):
        remote(
            solved_tx.at[0], solved_rx.at[groups + p], solved_send.at[groups + p], solved_recv.at[groups + p], right
        ).wait()

    each(1, groups, back_own)
    each(0, groups, back_next)

    def corrections(start, group, hot):
        rows = -(-groups // 8) * 8
        at_row = iota((rows, wide), 0)
        gathered = jnp.zeros((rows, wide), F32)
        for p in range(groups):
            gathered = jnp.where(at_row == p, jnp.broadcast_to(solved_rx[start + p], (rows, wide)), gathered)
        shape = (wide, vertices)
        slots = []
        inside = iota((rows, vertices), 0) == iota((rows, vertices), 1) // message
        for c in range(3):
            base = c * block + lax.rem(group, per_block) * message
            chosen = (iota(shape, 0) == base + lax.rem(iota(shape, 1), message)).astype(F32).astype(BF16)
            slots.append(
                jnp.sum(jnp.where(inside, stacked_exact(gathered, chosen, dot), 0.0), axis=0, keepdims=True)
            )
        slots = jnp.concatenate(slots + [jnp.zeros((5, vertices), F32)], axis=0)
        return stacked_exact(slots, hot, dot)

    own_correction = corrections(0, g, own_hot)
    next_correction = jnp.where(is_last, 0.0, corrections(groups, g_right, right_hot))
    rows = []
    for c in range(3):
        rows.append(jnp.broadcast_to(own_correction[c : c + 1], (8, vertices)))
        rows.append(jnp.broadcast_to(next_correction[c : c + 1], (8, vertices)))
    rows = jnp.where(vertex_mask, jnp.concatenate(rows, axis=0), 0.0)
    rows = times_right(rows, hatzp_ref[...])
    rows = jnp.concatenate([rows[16 * c : 16 * c + 16] for c in range(3)], axis=1)
    update = times_left(hatst_ref[...], rows)
    new_direction, beyond_new = [], []
    for c in range(3):
        part = update[:, c * lanes : (c + 1) * lanes]
        new_direction.append(own_direction[c] + keep * part[: 4 * ny])
        beyond_new.append(beyond_direction[c] + keep_right * part[4 * ny :])
        new_ref[c] = new_direction[c].reshape(4, ny, lanes)
    beyond_new = [jnp.where(is_last, 0.0, t) for t in beyond_new]
    gradients(widened([keep * t for t in new_direction], beyond_new), gvb, gvz)
    fluxes(False)
    image = divergence()
    for c in range(3):
        last_tx[c * ny : (c + 1) * ny, :] = image[4 * ny :, c * lanes : (c + 1) * lanes]
    copy_layer = remote(
        last_tx.at[pl.ds(0, 3 * ny)], last_rx.at[pl.ds(0, 3 * ny)], last_send.at[0], last_recv.at[0], right
    )
    copy_layer.start()
    own_last, beyond_last = settle(image, new_direction)
    low_sums, high_sums = restrict(widened(own_last, beyond_last))
    last_tx[3 * ny :, :] = high_sums
    copy_sums = remote(
        last_tx.at[pl.ds(3 * ny, 8)], last_rx.at[pl.ds(3 * ny, 8)], last_send.at[1], last_recv.at[1], right
    )
    copy_sums.start()
    for c in range(3):
        residual_ref[c, 1:] = own_last[c][ny:].reshape(3, ny, lanes)
    copy_layer.wait_recv()
    for c in range(3):
        arrived = jnp.where(is_first, 0.0, last_rx[c * ny : (c + 1) * ny, :])
        residual_ref[c, 0] = own_last[c][:ny] - keep[:ny] * arrived
    copy_sums.wait_recv()
    total = low_sums + jnp.where(is_first, 0.0, last_rx[3 * ny :, :])
    for c in range(3):
        for k in range(count_y):
            coarse_ref[c, 0, k : k + 1, :] = total[c : c + 1, k * count_z : (k + 1) * count_z]
    copy_state.wait_send()
    copy_halo.wait_send()
    copy_layer.wait_send()
    copy_sums.wait_send()


def shards(groups, members, state, direction, rhs, clamp, stiffness, coarse_owner, coarse_inverse):
    count_y, count_z = stiffness.shape[1:]
    ny, nz = 4 * count_y, 4 * count_z
    tables = [jnp.asarray(t) for t in constant_tables(count_y, count_z)]
    blocks, size = coarse_inverse.shape[1:3]
    wide = -(-size // 128) * 128
    vmem = pl.BlockSpec(memory_space=pltpu.VMEM)
    vertices = count_y * count_z
    new, residual, coarse = pl.pallas_call(
        functools.partial(kernel, groups, members),
        out_shape=(
            jax.ShapeDtypeStruct(state.shape, F32),
            jax.ShapeDtypeStruct(state.shape, F32),
            jax.ShapeDtypeStruct((3, 1, count_y, count_z), F32),
        ),
        in_specs=[vmem] * (7 + len(tables)),
        out_specs=(vmem, vmem, vmem),
        scratch_shapes=[
            pltpu.VMEM((4 * ny + 8, nz), F32),
            pltpu.VMEM((3, ny, nz), F32),
            pltpu.VMEM((4 * ny + 8, nz), F32),
            pltpu.VMEM((2, 8, vertices), F32),
            pltpu.VMEM((2 * groups, 8, vertices), F32),
            pltpu.VMEM((blocks, 1, wide), F32),
            pltpu.VMEM((2 * groups, 1, wide), F32),
            pltpu.VMEM((3 * ny + 8, nz), F32),
            pltpu.VMEM((3 * ny + 8, nz), F32),
            pltpu.VMEM((blocks, wide, wide), BF16),
            pltpu.VMEM((blocks, wide, wide), BF16),
            pltpu.VMEM((NQ, 256), F32),
            pltpu.VMEM((6 * NQ, 256), F32),
            pltpu.VMEM((3 * NQ, 256), F32),
            pltpu.VMEM((6 * NQ, 256), F32),
            pltpu.VMEM((3 * NQ, 256), F32),
            pltpu.VMEM((9, NQ, 256), F32),
            pltpu.VMEM((6, NQ, 256), F32),
            pltpu.VMEM((6 * NQ, 256), BF16),
            pltpu.VMEM((6 * NQ, 256), BF16),
            pltpu.VMEM((3 * NQ, 256), BF16),
            pltpu.VMEM((3 * NQ, 256), BF16),
            pltpu.SemaphoreType.DMA((2,)),
            pltpu.SemaphoreType.DMA((2,)),
            pltpu.SemaphoreType.DMA((2 * groups,)),
            pltpu.SemaphoreType.DMA((2 * groups,)),
            pltpu.SemaphoreType.DMA((2 * groups,)),
            pltpu.SemaphoreType.DMA((2 * groups,)),
            pltpu.SemaphoreType.DMA((2,)),
            pltpu.SemaphoreType.DMA((2,)),
        ],
        compiler_params=pltpu.CompilerParams(
            collective_id=0, has_side_effects=True, vmem_limit_bytes=40 * 1024 * 1024
        ),
    )(state, direction, rhs, clamp, stiffness, coarse_owner, coarse_inverse, *tables)
    return (new, residual, coarse)


def solution(mesh):
    in_specs = (
        P(None, ("grp", "mem"), None, None),
        P(None, ("grp", "mem"), None, None),
        P(None, ("grp", "mem"), None, None),
        P(("grp", "mem"), None),
        P(("grp", "mem"), None, None),
        P(("grp", "mem"), None),
        P(("grp", "mem"), None, None, None),
    )
    out_specs = (
        P(None, ("grp", "mem"), None, None),
        P(None, ("grp", "mem"), None, None),
        P(None, ("grp", "mem"), None, None),
    )
    body = functools.partial(shards, mesh.shape["grp"], mesh.shape["mem"])
    return jax.shard_map(body, mesh=mesh, in_specs=in_specs, out_specs=out_specs, check_vma=False)
```

time: 105 us -> 49.5 us (0.47)
  the two profiles are of different devices: /device:TPU:8 before, /device:TPU:0 now
where the time goes in v1:
time: 49.5 us; the launch traced here: 48.8 us
  Pallas kernels  30.3 us (61%)
  local copies, waits for them, and re-layouts  17.8 us (36%)
  between operations  0.67 us (1%)
    pallas_call x1, Pallas kernels, shards(): pl.pallas_call(functools.partial(kernel, groups, members), out_shape=(jax...  30.3 us
    unnamed x41, local copies, waits for them, and re-layouts  17.8 us

profile of v1, /device:TPU:0, one launch (start us, length us, event | category | flops | bytes accessed | tf_op | source)
XLA Modules:
  0.0 48.8 jit_solution(9987936186693364712)
XLA Ops:
  0.6 0.0 copy-start.15
  0.6 0.7 %copy-done.15 = bf16[16,256]{1,0:T(8,128)(2,1)S(1)} copy-done((bf16[16,256]{1,0:T(8,128)(2,1)S(1)}, bf16[16,256]{1,0:T(8,128)(2,1)}, u32[]{:S(2)}) %copy-start.15) | copy-done | bytes 8216
  1.3 0.0 copy-start
  1.3 1.0 %copy-done = f32[1,2,192,192]{3,2,1,0:T(8,128)S(1)} copy-done((f32[1,2,192,192]{3,2,1,0:T(8,128)S(1)}, f32[1,2,192,192]{3,2,1,0:T(8,128)}, u32[]{:S(2)}) %copy-start) | copy-done | bytes 294936
  2.3 0.0 copy-start.1
  2.3 0.9 %copy-done.1 = bf16[384,256]{1,0:T(8,128)(2,1)S(1)} copy-done((bf16[384,256]{1,0:T(8,128)(2,1)S(1)}, bf16[384,256]{1,0:T(8,128)(2,1)}, u32[]{:S(2)}) %copy-start.1) | copy-done | bytes 196632
  3.3 0.0 copy-start.2
  3.3 0.9 %copy-done.2 = bf16[384,256]{1,0:T(8,128)(2,1)S(1)} copy-done((bf16[384,256]{1,0:T(8,128)(2,1)S(1)}, bf16[384,256]{1,0:T(8,128)(2,1)}, u32[]{:S(2)}) %copy-start.2) | copy-done | bytes 196632
  4.2 0.0 copy-start.3
  4.2 0.9 %copy-done.3 = bf16[336,256]{1,0:T(8,128)(2,1)S(1)} copy-done((bf16[336,256]{1,0:T(8,128)(2,1)S(1)}, bf16[336,256]{1,0:T(8,128)(2,1)}, u32[]{:S(2)}) %copy-start.3) | copy-done | bytes 172056
  5.1 0.0 copy-start.4
  5.1 0.9 %copy-done.4 = bf16[80,1024]{1,0:T(8,128)(2,1)S(1)} copy-done((bf16[80,1024]{1,0:T(8,128)(2,1)S(1)}, bf16[80,1024]{1,0:T(8,128)(2,1)}, u32[]{:S(2)}) %copy-start.4) | copy-done | bytes 163864
  6.0 0.0 copy-start.5
  6.0 0.9 %copy-done.5 = bf16[256,256]{1,0:T(8,128)(2,1)S(1)} copy-done((bf16[256,256]{1,0:T(8,128)(2,1)S(1)}, bf16[256,256]{1,0:T(8,128)(2,1)}, u32[]{:S(2)}) %copy-start.5) | copy-done | bytes 131096
  6.9 0.0 copy-start.6
  6.9 0.9 %copy-done.6 = bf16[256,256]{1,0:T(8,128)(2,1)S(1)} copy-done((bf16[256,256]{1,0:T(8,128)(2,1)S(1)}, bf16[256,256]{1,0:T(8,128)(2,1)}, u32[]{:S(2)}) %copy-start.6) | copy-done | bytes 131096
  7.8 0.0 copy-start.7
  7.8 0.9 %copy-done.7 = f32[3,4,16,128]{3,2,1,0:T(8,128)S(1)} copy-done((f32[3,4,16,128]{3,2,1,0:T(8,128)S(1)}, f32[3,4,16,128]{3,2,1,0:T(8,128)}, u32[]{:S(2)}) %copy-start.7) | copy-done | bytes 98328
  8.7 0.9 %copy-done.8 = f32[3,4,16,128]{3,2,1,0:T(8,128)S(1)} copy-done((f32[3,4,16,128]{3,2,1,0:T(8,128)S(1)}, f32[3,4,16,128]{3,2,1,0:T(8,128)}, u32[]{:S(2)}) %copy-start.8) | copy-done | bytes 98328
  9.6 0.9 %copy-done.9 = f32[3,4,16,128]{3,2,1,0:T(8,128)S(1)} copy-done((f32[3,4,16,128]{3,2,1,0:T(8,128)S(1)}, f32[3,4,16,128]{3,2,1,0:T(8,128)}, u32[]{:S(2)}) %copy-start.9) | copy-done | bytes 98328
  10.5 0.9 %copy-done.10 = bf16[384,128]{1,0:T(8,128)(2,1)S(1)} copy-done((bf16[384,128]{1,0:T(8,128)(2,1)S(1)}, bf16[384,128]{1,0:T(8,128)(2,1)}, u32[]{:S(2)}) %copy-start.10) | copy-done | bytes 98328
  11.4 0.9 %copy-done.11 = bf16[384,128]{1,0:T(8,128)(2,1)S(1)} copy-done((bf16[384,128]{1,0:T(8,128)(2,1)S(1)}, bf16[384,128]{1,0:T(8,128)(2,1)}, u32[]{:S(2)}) %copy-start.11) | copy-done | bytes 98328
  12.3 0.8 %copy-done.12 = f32[112,4]{1,0:T(8,128)S(1)} copy-done((f32[112,4]{1,0:T(8,128)S(1)}, f32[112,4]{1,0:T(8,128)}, u32[]{:S(2)}) %copy-start.12) | copy-done | bytes 1816
  13.1 0.8 %copy-done.13 = f32[32,256]{1,0:T(8,128)S(1)} copy-done((f32[32,256]{1,0:T(8,128)S(1)}, f32[32,256]{1,0:T(8,128)}, u32[]{:S(2)}) %copy-start.13) | copy-done | bytes 32792
  13.9 0.7 %copy-done.14 = bf16[80,128]{1,0:T(8,128)(2,1)S(1)} copy-done((bf16[80,128]{1,0:T(8,128)(2,1)S(1)}, bf16[80,128]{1,0:T(8,128)(2,1)}, u32[]{:S(2)}) %copy-start.14) | copy-done | bytes 20504
  14.6 0.7 %copy-done.16 = s32[4,16]{1,0:T(4,128)S(1)} copy-done((s32[4,16]{1,0:T(4,128)S(1)}, s32[4,16]{1,0:T(4,128)}, u32[]{:S(2)}) %copy-start.16) | copy-done | bytes 280
  15.3 0.7 %copy-done.17 = f32[1,4,32]{2,1,0:T(4,128)S(1)} copy-done((f32[1,4,32]{2,1,0:T(4,128)S(1)}, f32[1,4,32]{2,1,0:T(4,128)}, u32[]{:S(2)}) %copy-start.17) | copy-done | bytes 536
  16.0 0.7 %copy-done.18 = s32[1,128]{1,0:T(1,128)S(1)} copy-done((s32[1,128]{1,0:T(1,128)S(1)}, s32[1,128]{1,0:T(1,128)}, u32[]{:S(2)}) %copy-start.18) | copy-done | bytes 536
  16.6 30.3 %shard_map.202 = (f32[3,4,16,128]{3,2,1,0:T(8,128)S(1)}, f32[3,4,16,128]{3,2,1,0:T(8,128)S(1)}, f32[3,1,4,32]{3,2,1,0:T(4,128)S(1)}) custom-call(f32[3,4,16,128]{3,2,1,0:T(8,128)S(1)} %copy-done.7, f32[3,4,16,128]{3,2,1,0:T(8,128)S(1)} %copy-done.8, f32[3,4,16,128]{3,2,1,0:T(8,128)S(1)} %copy-done.9, s32[4,16]{1,0:T(4,128)S(1)} %copy-done.16, ...), custom_call_target="tpu_custom_call" | custom-call | tf_op jit(solution)/shard_map/pallas_call | solution.py:597
  47.0 0.6 %copy.25 = f32[3,4,16,128]{3,2,1,0:T(8,128)} copy(f32[3,4,16,128]{3,2,1,0:T(8,128)S(1)} %get-tuple-element.6) | data formatting | bytes 196608
  47.6 0.6 %copy.26 = f32[3,4,16,128]{3,2,1,0:T(8,128)} copy(f32[3,4,16,128]{3,2,1,0:T(8,128)S(1)} %get-tuple-element.7) | data formatting | bytes 196608
  48.2 0.6 %copy.27 = f32[3,1,4,32]{3,2,1,0:T(4,128)} copy(f32[3,1,4,32]{3,2,1,0:T(4,128)S(1)} %get-tuple-element.8) | data formatting | bytes 3072
  (10 shorter events, 0.0 us)
Async XLA Ops:
  0.6 0.7 %copy-start.15 = (bf16[16,256]{1,0:T(8,128)(2,1)S(1)}, bf16[16,256]{1,0:T(8,128)(2,1)}, u32[]{:S(2)}) copy-start(bf16[16,256]{1,0:T(8,128)(2,1)} %constant.30.clone.hats_ref) | copy-start | bytes 24580
  1.3 1.0 %copy-start = (f32[1,2,192,192]{3,2,1,0:T(8,128)S(1)}, f32[1,2,192,192]{3,2,1,0:T(8,128)}, u32[]{:S(2)}) copy-start(f32[1,2,192,192]{3,2,1,0:T(8,128)} %inverse_ref.1) | copy-start | bytes 884740
  2.3 0.9 %copy-start.1 = (bf16[384,256]{1,0:T(8,128)(2,1)S(1)}, bf16[384,256]{1,0:T(8,128)(2,1)}, u32[]{:S(2)}) copy-start(bf16[384,256]{1,0:T(8,128)(2,1)} %constant.26.clone.dz_ref) | copy-start | bytes 589828
  3.3 0.9 %copy-start.2 = (bf16[384,256]{1,0:T(8,128)(2,1)S(1)}, bf16[384,256]{1,0:T(8,128)(2,1)}, u32[]{:S(2)}) copy-start(bf16[384,256]{1,0:T(8,128)(2,1)} %constant.25.clone.bz_ref) | copy-start | bytes 589828
  4.2 0.9 %copy-start.3 = (bf16[336,256]{1,0:T(8,128)(2,1)S(1)}, bf16[336,256]{1,0:T(8,128)(2,1)}, u32[]{:S(2)}) copy-start(bf16[336,256]{1,0:T(8,128)(2,1)} %constant.24.clone.cross_ref) | copy-start | bytes 516100
  5.1 0.9 %copy-start.4 = (bf16[80,1024]{1,0:T(8,128)(2,1)S(1)}, bf16[80,1024]{1,0:T(8,128)(2,1)}, u32[]{:S(2)}) copy-start(bf16[80,1024]{1,0:T(8,128)(2,1)} %constant.29.clone.crosst_ref) | copy-start | bytes 491524
  6.0 0.9 %copy-start.5 = (bf16[256,256]{1,0:T(8,128)(2,1)S(1)}, bf16[256,256]{1,0:T(8,128)(2,1)}, u32[]{:S(2)}) copy-start(bf16[256,256]{1,0:T(8,128)(2,1)} %constant.28.clone.dzt_ref) | copy-start | bytes 393220
  6.9 0.9 %copy-start.6 = (bf16[256,256]{1,0:T(8,128)(2,1)S(1)}, bf16[256,256]{1,0:T(8,128)(2,1)}, u32[]{:S(2)}) copy-start(bf16[256,256]{1,0:T(8,128)(2,1)} %constant.27.clone.bzt_ref) | copy-start | bytes 393220
  7.8 0.9 %copy-start.7 = (f32[3,4,16,128]{3,2,1,0:T(8,128)S(1)}, f32[3,4,16,128]{3,2,1,0:T(8,128)}, u32[]{:S(2)}) copy-start(f32[3,4,16,128]{3,2,1,0:T(8,128)} %state_ref.1) | copy-start | bytes 294916
  8.7 0.9 %copy-start.8 = (f32[3,4,16,128]{3,2,1,0:T(8,128)S(1)}, f32[3,4,16,128]{3,2,1,0:T(8,128)}, u32[]{:S(2)}) copy-start(f32[3,4,16,128]{3,2,1,0:T(8,128)} %direction_ref.1) | copy-start | bytes 294916
  9.6 0.9 %copy-start.9 = (f32[3,4,16,128]{3,2,1,0:T(8,128)S(1)}, f32[3,4,16,128]{3,2,1,0:T(8,128)}, u32[]{:S(2)}) copy-start(f32[3,4,16,128]{3,2,1,0:T(8,128)} %rhs_ref.1) | copy-start | bytes 294916
  10.5 0.9 %copy-start.10 = (bf16[384,128]{1,0:T(8,128)(2,1)S(1)}, bf16[384,128]{1,0:T(8,128)(2,1)}, u32[]{:S(2)}) copy-start(bf16[384,128]{1,0:T(8,128)(2,1)} %constant.32.clone.hatzp_ref) | copy-start | bytes 294916
  11.4 0.9 %copy-start.11 = (bf16[384,128]{1,0:T(8,128)(2,1)S(1)}, bf16[384,128]{1,0:T(8,128)(2,1)}, u32[]{:S(2)}) copy-start(bf16[384,128]{1,0:T(8,128)(2,1)} %constant.31.clone.hatz_ref) | copy-start | bytes 294916
  12.3 0.8 %copy-start.12 = (f32[112,4]{1,0:T(8,128)S(1)}, f32[112,4]{1,0:T(8,128)}, u32[]{:S(2)}) copy-start(f32[112,4]{1,0:T(8,128)} %constant.34.clone.spready_ref) | copy-start | bytes 5380
  13.1 0.8 %copy-start.13 = (f32[32,256]{1,0:T(8,128)S(1)}, f32[32,256]{1,0:T(8,128)}, u32[]{:S(2)}) copy-start(f32[32,256]{1,0:T(8,128)} %constant.35.clone.spreadz_ref) | copy-start | bytes 98308
  13.9 0.7 %copy-start.14 = (bf16[80,128]{1,0:T(8,128)(2,1)S(1)}, bf16[80,128]{1,0:T(8,128)(2,1)}, u32[]{:S(2)}) copy-start(bf16[80,128]{1,0:T(8,128)(2,1)} %constant.33.clone.hatst_ref) | copy-start | bytes 61444
  14.6 0.7 %copy-start.16 = (s32[4,16]{1,0:T(4,128)S(1)}, s32[4,16]{1,0:T(4,128)}, u32[]{:S(2)}) copy-start(s32[4,16]{1,0:T(4,128)} %clamp_ref.1) | copy-start | bytes 772
  15.3 0.7 %copy-start.17 = (f32[1,4,32]{2,1,0:T(4,128)S(1)}, f32[1,4,32]{2,1,0:T(4,128)}, u32[]{:S(2)}) copy-start(f32[1,4,32]{2,1,0:T(4,128)} %stiff_ref.1) | copy-start | bytes 1540
  16.0 0.7 %copy-start.18 = (s32[1,128]{1,0:T(1,128)S(1)}, s32[1,128]{1,0:T(1,128)}, u32[]{:S(2)}) copy-start(s32[1,128]{1,0:T(1,128)} %owner_ref.1) | copy-start | bytes 1540

commit v2 on v1

--- a/solution.py
+++ b/solution.py
@@ -15,6 +15,7 @@
 MESH = pl.DeviceIdType.MESH
 F32 = jnp.float32
 BF16 = jnp.bfloat16
+INPUTS = 18
 NQ = 112
 
 
@@ -107,8 +108,7 @@
     spread_z = padded(np.kron(np.eye(count_z), weights[None]), 1, 256)
     return (
         left_table(cross),
-        right_table(bz.T),
-        right_table(dz.T),
+        right_table(np.concatenate([bz.T, dz.T], axis=1)),
         np.concatenate(halves(bz), axis=1),
         np.concatenate(halves(dz), axis=1),
         left_table(cross.T),
@@ -172,62 +172,48 @@
         lax.fori_loop(low, high, step, 0)
 
 
-def kernel(
-    groups,
-    members,
-    state_ref,
-    direction_ref,
-    rhs_ref,
-    clamp_ref,
-    stiff_ref,
-    owner_ref,
-    inverse_ref,
-    cross_ref,
-    bz_ref,
-    dz_ref,
-    bzt_ref,
-    dzt_ref,
-    crosst_ref,
-    hats_ref,
-    hatz_ref,
-    hatzp_ref,
-    hatst_ref,
-    spready_ref,
-    spreadz_ref,
-    new_ref,
-    residual_ref,
-    coarse_ref,
-    halo_tx,
-    halo_state,
-    halo_rx,
-    sums_tx,
-    sums_rx,
-    solved_tx,
-    solved_rx,
-    last_tx,
-    last_rx,
-    inv_high,
-    inv_low,
-    weight,
-    gsb,
-    gsz,
-    gvb,
-    gvz,
-    deform_s,
-    stress_s,
-    fbh,
-    fbl,
-    fzh,
-    fzl,
-    halo_send,
-    halo_recv,
-    sums_send,
-    sums_recv,
-    solved_send,
-    solved_recv,
-    last_send,
-    last_recv,
-):
+def kernel(groups, members, *refs):
+    sources, outputs = refs[:INPUTS], refs[INPUTS : INPUTS + 3]
+    local, scratch = refs[INPUTS + 3 : 2 * INPUTS + 3], refs[2 * INPUTS + 3 :]
+    state_ref, direction_ref, rhs_ref, clamp_ref, stiff_ref, owner_ref, inverse_ref = local[:7]
+    spready_ref, spreadz_ref = local[16:]
+    new_ref, residual_ref, coarse_ref = scratch[:3]
+    narrow = scratch[3:12]
+    cross_ref, bdz_ref, bzt_ref, dzt_ref, crosst_ref, hats_ref, hatz_ref, hatzp_ref, hatst_ref = narrow
+    (
+        halo_tx,
+        halo_state,
+        halo_rx,
+        sums_tx,
+        sums_rx,
+        solved_tx,
+        solved_rx,
+        last_tx,
+        last_rx,
+        inv_high,
+        inv_low,
+        weight,
+        gsb,
+        gsz,
+        gvb,
+        gvz,
+        deform_s,
+        stress_s,
+        fbh,
+        fbl,
+        fzh,
+        fzl,
+        halo_send,
+        halo_recv,
+        sums_send,
+        sums_recv,
+        solved_send,
+        solved_recv,
+        last_send,
+        last_recv,
+        load_sem,
+        store_sem,
+    ) = scratch[12:]
     count_y, count_z = stiff_ref.shape[1:]
     ny = 4 * count_y
     vertices = count_y * count_z
@@ -252,11 +238,22 @@
     def greet(p, member):
         pl.semaphore_signal(barrier, inc=1, device_id=(p, member), device_id_type=MESH)
 
-    sums_rx[...] = jnp.zeros_like(sums_rx)
     greet(g_left, m_left)
     each(1, groups, lambda d: greet(lax.rem(g_left + d, groups), m_left))
     each(0, groups, lambda d: greet(lax.rem(g_right + d, groups), m_right))
     each(1, groups, lambda d: greet(lax.rem(g + d, groups), m))
+    loads = [pltpu.make_async_copy(a, b, load_sem.at[i]) for i, (a, b) in enumerate(zip(sources, local))]
+    order = [3, 5, 1, 0, 6, 4, 16, 17, 8, 7]
+    for i in order + [i for i in range(INPUTS) if i not in order]:
+        loads[i].start()
+
+    def loaded(*which):
+        for i in which:
+            loads[i].wait()
+            if 7 <= i < 16:
+                narrow[i - 7][...] = local[i][...].astype(BF16)
+
+    loaded(3, 5, 1)
 
     eye = iota((ny, ny), 0) == iota((ny, ny), 1)
     clamp_rows = []
@@ -272,6 +269,9 @@
     halo_tx[4 * ny : 4 * ny + 8, :] = jnp.broadcast_to(owner_ref[...].astype(F32), (8, vertices))
     pl.semaphore_wait(barrier, 3 * groups - 1)
 
+    def along_z(parts):
+        return times_right(jnp.concatenate(parts, axis=0), bdz_ref[...])
+
     left = (g_left, m_left)
     right = (g_right, m_right)
 
@@ -280,11 +280,18 @@
             src_ref=src, dst_ref=dst, send_sem=send, recv_sem=recv, device_id=device, device_id_type=MESH
         )
 
-    copy_state = remote(state_ref.at[:, 0], halo_state, halo_send.at[0], halo_recv.at[0], left)
+    copy_state = remote(sources[0].at[:, 0], halo_state, halo_send.at[0], halo_recv.at[0], left)
     copy_state.start()
     copy_halo = remote(halo_tx, halo_rx, halo_send.at[1], halo_recv.at[1], left)
     copy_halo.start()
 
+    loaded(0, 8)
+    own_state = [state_ref[c].reshape(4 * ny, lanes) for c in range(3)]
+    own_direction = [direction_ref[c].reshape(4 * ny, lanes) for c in range(3)]
+    state_z = along_z(own_state)
+    direction_z = along_z([keep * t for t in own_direction])
+    sums_rx[:, 4:, :] = jnp.zeros((2 * groups, 4, vertices), F32)
+    loaded(6, 4, 16, 17)
     inv_high[...] = jnp.zeros_like(inv_high)
     inv_low[...] = jnp.zeros_like(inv_low)
     for b in range(blocks):
@@ -297,21 +304,53 @@
     weight[...] = jnp.dot(along_y, spreadz_ref[...], precision=HIGHEST, preferred_element_type=F32)
     own_hot = (owner_ref[...] == iota((vertices, vertices), 0)).astype(F32).astype(BF16)
 
-    def gradients(field, to_b, to_z):
-        parts = times_left(cross_ref[...], field)
-        plain = jnp.concatenate([parts[: 2 * NQ, c * lanes : (c + 1) * lanes] for c in range(3)], axis=0)
-        sloped = jnp.concatenate([parts[2 * NQ :, c * lanes : (c + 1) * lanes] for c in range(3)], axis=0)
-        to_b[...] = times_right(plain, bz_ref[...])
-        to_z[...] = times_right(sloped, dz_ref[...])
-
-    def load_change(from_b, from_z, r, s):
+    wide = inv_high.shape[2]
+    pick = (
+        iota((vertices, wide), 0) == g * message + lax.rem(iota((vertices, wide), 1), message)
+    ).astype(F32).astype(BF16)
+    shape = (groups * 8, wide)
+    row, lane = iota(shape, 0), iota(shape, 1)
+    pick_mask = (
+        (lane // block == lax.rem(row, 8))
+        & (lax.rem(lane, block) // message == lax.rem(row // 8, per_block))
+        & (lane < size)
+    )
+    owner_rows = -(-groups // 8) * 8
+
+    def choices(owner, group):
+        place = lax.rem(group, per_block) * message + lax.rem(owner, message)
+        rows = iota((wide, vertices), 0)
+        chosen = jnp.concatenate([rows == c * block + place for c in range(3)], axis=1)
+        return chosen.astype(F32).astype(BF16), iota((owner_rows, vertices), 0) == owner // message
+
+    own_choices = choices(owner_ref[...], g)
+
+    def gradients(own, beyond, to_b, to_z):
+        parts = []
+        for first in (0, 256):
+            columns = [
+                jnp.concatenate(
+                    [
+                        own[c * 4 * ny : (c + 1) * 4 * ny, first : first + 256],
+                        beyond[c * ny : (c + 1) * ny, first : first + 256],
+                    ],
+                    axis=0,
+                )
+                for c in range(3)
+            ]
+            parts.append(jnp.concatenate(columns, axis=1))
+        to_b[...] = times_left(cross_ref[: 2 * NQ, :], parts[0])
+        to_z[...] = times_left(cross_ref[2 * NQ :, :], parts[1])
+
+    def load_change(from_b, from_z, r, half):
         change = []
         for c in range(3):
+            s = pl.ds(c * 256 + half * 128, 128)
             change.append(
                 [
-                    from_b[pl.ds(pl.multiple_of(c * 2 * NQ + r, 16), 16), s],
-                    from_b[pl.ds(pl.multiple_of(c * 2 * NQ + NQ + r, 16), 16), s],
-                    from_z[pl.ds(pl.multiple_of(c * NQ + r, 16), 16), s],
+                    from_b[pl.ds(r, 16), s],
+                    from_b[pl.ds(pl.multiple_of(NQ + r, 16), 16), s],
+                    from_z[pl.ds(r, 16), s],
                 ]
             )
         return change
@@ -325,7 +364,7 @@
                 s = pl.ds(half * 128, 128)
                 w = weight[pl.ds(r, 16), s]
                 if first:
-                    grad = load_change(gsb, gsz, r, s)
+                    grad = load_change(gsb, gsz, r, half)
                     deform = [[grad[c][a] + 1.0 if c == a else grad[c][a] for a in range(3)] for c in range(3)]
                     cg = [sum(deform[k][a] * deform[k][b] for k in range(3)) for a, b in pairs]
                     trace = (0.5 * LAME_FIRST) * (cg[0] + cg[1] + cg[2]) - 1.5 * LAME_FIRST
@@ -339,7 +378,7 @@
                 else:
                     deform = [[deform_s[3 * c + a, pl.ds(r, 16), s] for a in range(3)] for c in range(3)]
                     stress = [stress_s[k, pl.ds(r, 16), s] for k in range(6)]
-                change = load_change(gvb, gvz, r, s)
+                change = load_change(gvb, gvz, r, half)
                 diagonal = [sum(deform[k][a] * change[k][a] for k in range(3)) for a in range(3)]
                 trace = LAME_FIRST * (diagonal[0] + diagonal[1] + diagonal[2])
                 moved = [w * (2.0 * LAME_SHEAR * t + trace) for t in diagonal]
@@ -393,19 +432,19 @@
     def widened(own, beyond):
         return jnp.concatenate([jnp.concatenate([own[c], beyond[c]], axis=0) for c in range(3)], axis=1)
 
-    own_state = [state_ref[c].reshape(4 * ny, lanes) for c in range(3)]
-    own_direction = [direction_ref[c].reshape(4 * ny, lanes) for c in range(3)]
+    loaded(*[i for i in range(INPUTS) if i not in (3, 5, 1, 0, 8, 6, 4, 16, 17)])
     own_rhs = [rhs_ref[c].reshape(4 * ny, lanes) for c in range(3)]
 
     copy_state.wait_recv()
     beyond_state = [jnp.where(is_last, 0.0, halo_state[c]) for c in range(3)]
-    gradients(widened(own_state, beyond_state), gsb, gsz)
+    gradients(state_z, along_z(beyond_state), gsb, gsz)
     copy_halo.wait_recv()
     beyond_direction = [jnp.where(is_last, 0.0, halo_rx[c * ny : (c + 1) * ny, :]) for c in range(3)]
     keep_right = halo_rx[3 * ny : 4 * ny, :]
     owner_right = halo_rx[4 * ny : 4 * ny + 1, :].astype(jnp.int32)
     right_hot = (owner_right == iota((vertices, vertices), 0)).astype(F32).astype(BF16)
-    gradients(widened([keep * own_direction[c] for c in range(3)], beyond_direction), gvb, gvz)
+    gradients(direction_z, along_z(beyond_direction), gvb, gvz)
+    right_choices = choices(owner_right, g_right)
     fluxes(True)
     image = divergence()
 
@@ -461,22 +500,9 @@
     each(1, groups, got_own)
     each(0, groups, got_next)
 
-    wide = inv_high.shape[2]
     received = sums_rx[:groups] + sums_rx[groups:]
     received = received.reshape(groups * 8, vertices)
-    pick = (
-        iota((vertices, wide), 0) == g * message + lax.rem(iota((vertices, wide), 1), message)
-    ).astype(F32).astype(BF16)
-    placed = stacked_exact(received, pick, dot)
-    shape = (groups * 8, wide)
-    row, lane = iota(shape, 0), iota(shape, 1)
-    placed = jnp.where(
-        (lane // block == lax.rem(row, 8))
-        & (lax.rem(lane, block) // message == lax.rem(row // 8, per_block))
-        & (lane < size),
-        placed,
-        0.0,
-    )
+    placed = jnp.where(pick_mask, stacked_exact(received, pick, dot), 0.0)
     vectors = [
         jnp.sum(placed[b * per_block * 8 : (b + 1) * per_block * 8], axis=0, keepdims=True) for b in range(blocks)
     ]
@@ -518,30 +544,21 @@
     each(1, groups, back_own)
     each(0, groups, back_next)
 
-    def corrections(start, group, hot):
-        rows = -(-groups // 8) * 8
-        at_row = iota((rows, wide), 0)
-        gathered = jnp.zeros((rows, wide), F32)
+    def corrections(start, chosen, mask):
+        at_row = iota((owner_rows, wide), 0)
+        gathered = jnp.zeros((owner_rows, wide), F32)
         for p in range(groups):
-            gathered = jnp.where(at_row == p, jnp.broadcast_to(solved_rx[start + p], (rows, wide)), gathered)
-        shape = (wide, vertices)
-        slots = []
-        inside = iota((rows, vertices), 0) == iota((rows, vertices), 1) // message
-        for c in range(3):
-            base = c * block + lax.rem(group, per_block) * message
-            chosen = (iota(shape, 0) == base + lax.rem(iota(shape, 1), message)).astype(F32).astype(BF16)
-            slots.append(
-                jnp.sum(jnp.where(inside, stacked_exact(gathered, chosen, dot), 0.0), axis=0, keepdims=True)
-            )
-        slots = jnp.concatenate(slots + [jnp.zeros((5, vertices), F32)], axis=0)
-        return stacked_exact(slots, hot, dot)
-
-    own_correction = corrections(0, g, own_hot)
-    next_correction = jnp.where(is_last, 0.0, corrections(groups, g_right, right_hot))
+            gathered = jnp.where(at_row == p, jnp.broadcast_to(solved_rx[start + p], gathered.shape), gathered)
+        values = stacked_exact(gathered, chosen, dot)
+        values = [values[:, c * vertices : (c + 1) * vertices] for c in range(3)]
+        return [jnp.sum(jnp.where(mask, t, 0.0), axis=0, keepdims=True) for t in values]
+
+    own_correction = corrections(0, *own_choices)
+    next_correction = [jnp.where(is_last, 0.0, t) for t in corrections(groups, *right_choices)]
     rows = []
     for c in range(3):
-        rows.append(jnp.broadcast_to(own_correction[c : c + 1], (8, vertices)))
-        rows.append(jnp.broadcast_to(next_correction[c : c + 1], (8, vertices)))
+        rows.append(jnp.broadcast_to(own_correction[c], (8, vertices)))
+        rows.append(jnp.broadcast_to(next_correction[c], (8, vertices)))
     rows = jnp.where(vertex_mask, jnp.concatenate(rows, axis=0), 0.0)
     rows = times_right(rows, hatzp_ref[...])
     rows = jnp.concatenate([rows[16 * c : 16 * c + 16] for c in range(3)], axis=1)
@@ -552,8 +569,10 @@
         new_direction.append(own_direction[c] + keep * part[: 4 * ny])
         beyond_new.append(beyond_direction[c] + keep_right * part[4 * ny :])
         new_ref[c] = new_direction[c].reshape(4, ny, lanes)
+    store_new = pltpu.make_async_copy(new_ref, outputs[0], store_sem.at[0])
+    store_new.start()
     beyond_new = [jnp.where(is_last, 0.0, t) for t in beyond_new]
-    gradients(widened([keep * t for t in new_direction], beyond_new), gvb, gvz)
+    gradients(along_z([keep * t for t in new_direction]), along_z(beyond_new), gvb, gvz)
     fluxes(False)
     image = divergence()
     for c in range(3):
@@ -571,29 +590,48 @@
     copy_sums.start()
     for c in range(3):
         residual_ref[c, 1:] = own_last[c][ny:].reshape(3, ny, lanes)
+    store_rest = pltpu.make_async_copy(residual_ref.at[:, 1:], outputs[1].at[:, 1:], store_sem.at[1])
+    store_rest.start()
     copy_layer.wait_recv()
     for c in range(3):
         arrived = jnp.where(is_first, 0.0, last_rx[c * ny : (c + 1) * ny, :])
         residual_ref[c, 0] = own_last[c][:ny] - keep[:ny] * arrived
+    store_first = pltpu.make_async_copy(residual_ref.at[:, 0], outputs[1].at[:, 0], store_sem.at[2])
+    store_first.start()
     copy_sums.wait_recv()
     total = low_sums + jnp.where(is_first, 0.0, last_rx[3 * ny :, :])
     for c in range(3):
         for k in range(count_y):
             coarse_ref[c, 0, k : k + 1, :] = total[c : c + 1, k * count_z : (k + 1) * count_z]
+    store_coarse = pltpu.make_async_copy(coarse_ref, outputs[2], store_sem.at[3])
+    store_coarse.start()
+    store_new.wait()
+    store_rest.wait()
+    store_first.wait()
+    store_coarse.wait()
     copy_state.wait_send()
     copy_halo.wait_send()
     copy_layer.wait_send()
     copy_sums.wait_send()
 
 
+def write_out(new, residual, coarse, new_out, residual_out, coarse_out, sems):
+    pairs = ((new, new_out), (residual, residual_out), (coarse, coarse_out))
+    copies = [pltpu.make_async_copy(a, b, sems.at[i]) for i, (a, b) in enumerate(pairs)]
+    for copy in copies:
+        copy.start()
+    for copy in copies:
+        copy.wait()
+
+
 def shards(groups, members, state, direction, rhs, clamp, stiffness, coarse_owner, coarse_inverse):
     count_y, count_z = stiffness.shape[1:]
     ny, nz = 4 * count_y, 4 * count_z
-    tables = [jnp.asarray(t) for t in constant_tables(count_y, count_z)]
+    tables = [jnp.asarray(t.astype(np.float32)) for t in constant_tables(count_y, count_z)]
     blocks, size = coarse_inverse.shape[1:3]
     wide = -(-size // 128) * 128
-    vmem = pl.BlockSpec(memory_space=pltpu.VMEM)
     vertices = count_y * count_z
+    operands = [state, direction, rhs, clamp, stiffness, coarse_owner, coarse_inverse, *tables]
     new, residual, coarse = pl.pallas_call(
         functools.partial(kernel, groups, members),
         out_shape=(
@@ -601,9 +639,12 @@
             jax.ShapeDtypeStruct(state.shape, F32),
             jax.ShapeDtypeStruct((3, 1, count_y, count_z), F32),
         ),
-        in_specs=[vmem] * (7 + len(tables)),
-        out_specs=(vmem, vmem, vmem),
-        scratch_shapes=[
+        in_specs=[pl.BlockSpec(memory_space=pl.ANY)] * INPUTS,
+        out_specs=[pl.BlockSpec(memory_space=pl.ANY)] * 3,
+        scratch_shapes=[pltpu.VMEM(t.shape, t.dtype) for t in operands]
+        + [pltpu.VMEM(t.shape, F32) for t in (state, state, jnp.zeros((3, 1, count_y, count_z), F32))]
+        + [pltpu.VMEM(t.shape, BF16) for t in tables[:9]]
+        + [
             pltpu.VMEM((4 * ny + 8, nz), F32),
             pltpu.VMEM((3, ny, nz), F32),
             pltpu.VMEM((4 * ny + 8, nz), F32),
@@ -616,10 +657,10 @@
             pltpu.VMEM((blocks, wide, wide), BF16),
             pltpu.VMEM((blocks, wide, wide), BF16),
             pltpu.VMEM((NQ, 256), F32),
-            pltpu.VMEM((6 * NQ, 256), F32),
-            pltpu.VMEM((3 * NQ, 256), F32),
-            pltpu.VMEM((6 * NQ, 256), F32),
-            pltpu.VMEM((3 * NQ, 256), F32),
+            pltpu.VMEM((2 * NQ, 768), F32),
+            pltpu.VMEM((NQ, 768), F32),
+            pltpu.VMEM((2 * NQ, 768), F32),
+            pltpu.VMEM((NQ, 768), F32),
             pltpu.VMEM((9, NQ, 256), F32),
             pltpu.VMEM((6, NQ, 256), F32),
             pltpu.VMEM((6 * NQ, 256), BF16),
@@ -634,12 +675,21 @@
             pltpu.SemaphoreType.DMA((2 * groups,)),
             pltpu.SemaphoreType.DMA((2,)),
             pltpu.SemaphoreType.DMA((2,)),
+            pltpu.SemaphoreType.DMA((INPUTS,)),
+            pltpu.SemaphoreType.DMA((4,)),
         ],
         compiler_params=pltpu.CompilerParams(
-            collective_id=0, has_side_effects=True, vmem_limit_bytes=40 * 1024 * 1024
+            collective_id=0, has_side_effects=True, vmem_limit_bytes=56 * 1024 * 1024
         ),
-    )(state, direction, rhs, clamp, stiffness, coarse_owner, coarse_inverse, *tables)
-    return (new, residual, coarse)
+    )(*operands)
+    return pl.pallas_call(
+        write_out,
+        out_shape=tuple(jax.ShapeDtypeStruct(t.shape, F32) for t in (new, residual, coarse)),
+        in_specs=[pl.BlockSpec(memory_space=pl.ANY)] * 3,
+        out_specs=[pl.BlockSpec(memory_space=pl.ANY)] * 3,
+        scratch_shapes=[pltpu.SemaphoreType.DMA((3,))],
+        compiler_params=pltpu.CompilerParams(vmem_limit_bytes=56 * 1024 * 1024),
+    )(new, residual, coarse)
 
 
 def solution(mesh):

time: 49.5 us -> 38.7 us (0.78)
  local copies, waits for them, and re-layouts: 17.8 us -> 0 us
  Pallas kernels: 30.3 us -> 37.9 us
    unnamed x41 -> x0, local copies, waits for them, and re-layouts: 17.8 us -> none
    pallas_call x0 -> x1, Pallas kernels: none -> 7.27 us  [shards(): pl.pallas_call(write_out, out_shape=tuple((jax.ShapeDtypeStruct(t.shape,...]
where the time goes in v2:
time: 38.7 us; the launch traced here: 38.5 us
  Pallas kernels  37.9 us (98%)
  between operations  0.64 us (2%)
    pallas_call x1, Pallas kernels, shards(): pl.pallas_call(functools.partial(kernel, groups, members), out_shape=(jax...  30.6 us
    pallas_call x1, Pallas kernels, shards(): pl.pallas_call(write_out, out_shape=tuple((jax.ShapeDtypeStruct(t.shape,...  7.27 us

profile of v2, /device:TPU:0, one launch (start us, length us, event | category | flops | bytes accessed | tf_op | source)
XLA Modules:
  0.0 38.5 jit_solution(3572213209849395683)
XLA Ops:
  0.6 30.6 %shard_map.193 = (f32[3,4,16,128]{3,2,1,0:T(8,128)}, f32[3,4,16,128]{3,2,1,0:T(8,128)}, f32[3,1,4,32]{3,2,1,0:T(4,128)}) custom-call(f32[3,4,16,128]{3,2,1,0:T(8,128)} %refs_0_.1, f32[3,4,16,128]{3,2,1,0:T(8,128)} %refs_1_.1, f32[3,4,16,128]{3,2,1,0:T(8,128)} %refs_2_.1, s32[4,16]{1,0:T(4,128)} %refs_3_.1, f32[1,4,32]{2,1,0:T(4,128)} %refs_4_.1, ...), custom_call_target="tpu_custom_call" | custom-call | tf_op jit(solution)/shard_map/pallas_call | solution.py:635
  31.2 7.3 %shard_map.194 = (f32[3,4,16,128]{3,2,1,0:T(8,128)}, f32[3,4,16,128]{3,2,1,0:T(8,128)}, f32[3,1,4,32]{3,2,1,0:T(4,128)}) custom-call(f32[3,4,16,128]{3,2,1,0:T(8,128)} %get-tuple-element.6.new, f32[3,4,16,128]{3,2,1,0:T(8,128)} %get-tuple-element.7.residual, f32[3,1,4,32]{3,2,1,0:T(4,128)} %get-tuple-element.8.coarse), custom_call_target="tpu_custom_call" | custom-call | tf_op jit(solution)/shard_map/pallas_call | solution.py:685

commit v3 on v2

--- a/solution.py
+++ b/solution.py
@@ -181,7 +181,8 @@
     narrow = scratch[3:12]
     cross_ref, bdz_ref, bzt_ref, dzt_ref, crosst_ref, hats_ref, hatz_ref, hatzp_ref, hatst_ref = narrow
     (
-        halo_tx,
+        halo_clamp,
+        halo_owner,
         halo_state,
         halo_rx,
         sums_tx,
@@ -253,20 +254,6 @@
             if 7 <= i < 16:
                 narrow[i - 7][...] = local[i][...].astype(BF16)
 
-    loaded(3, 5, 1)
-
-    eye = iota((ny, ny), 0) == iota((ny, ny), 1)
-    clamp_rows = []
-    for x in range(4):
-        row = jnp.broadcast_to(clamp_ref[x : x + 1, :].astype(F32), (ny, ny))
-        clamp_rows.append(jnp.sum(jnp.where(eye, row, 0.0), axis=1, keepdims=True))
-    clamped = jnp.concatenate(clamp_rows, axis=0)
-    lanes = 4 * count_z
-    keep = jnp.where(iota((4 * ny, lanes), 1) == 0, 1.0 - clamped, 1.0)
-    for c in range(3):
-        halo_tx[c * ny : (c + 1) * ny, :] = keep[:ny] * direction_ref[c, 0]
-    halo_tx[3 * ny : 4 * ny, :] = keep[:ny]
-    halo_tx[4 * ny : 4 * ny + 8, :] = jnp.broadcast_to(owner_ref[...].astype(F32), (8, vertices))
     pl.semaphore_wait(barrier, 3 * groups - 1)
 
     def along_z(parts):
@@ -280,10 +267,34 @@
             src_ref=src, dst_ref=dst, send_sem=send, recv_sem=recv, device_id=device, device_id_type=MESH
         )
 
-    copy_state = remote(sources[0].at[:, 0], halo_state, halo_send.at[0], halo_recv.at[0], left)
-    copy_state.start()
-    copy_halo = remote(halo_tx, halo_rx, halo_send.at[1], halo_recv.at[1], left)
-    copy_halo.start()
+    halo = [
+        remote(a, b, halo_send.at[i], halo_recv.at[i], left)
+        for i, (a, b) in enumerate(
+            (
+                (sources[0].at[:, 0], halo_state),
+                (sources[1].at[:, 0], halo_rx),
+                (sources[3], halo_clamp),
+                (sources[5], halo_owner),
+            )
+        )
+    ]
+
+    @pl.when(jnp.logical_not(is_first))
+    def _():
+        for copy in halo:
+            copy.start()
+
+    def clamp_column(ref, x):
+        row = jnp.broadcast_to(ref[x : x + 1, :].astype(F32), (ny, ny))
+        return jnp.sum(jnp.where(iota((ny, ny), 0) == iota((ny, ny), 1), row, 0.0), axis=1, keepdims=True)
+
+    def keep_of(column):
+        shape = (column.shape[0], lanes)
+        return jnp.where(iota(shape, 1) == 0, jnp.broadcast_to(1.0 - column, shape), 1.0)
+
+    lanes = 4 * count_z
+    loaded(3, 5, 1)
+    keep = keep_of(jnp.concatenate([clamp_column(clamp_ref, x) for x in range(4)], axis=0))
 
     loaded(0, 8)
     own_state = [state_ref[c].reshape(4 * ny, lanes) for c in range(3)]
@@ -291,13 +302,7 @@
     state_z = along_z(own_state)
     direction_z = along_z([keep * t for t in own_direction])
     sums_rx[:, 4:, :] = jnp.zeros((2 * groups, 4, vertices), F32)
-    loaded(6, 4, 16, 17)
-    inv_high[...] = jnp.zeros_like(inv_high)
-    inv_low[...] = jnp.zeros_like(inv_low)
-    for b in range(blocks):
-        high, low = split(inverse_ref[0, b])
-        inv_high[b, :size, :size] = high
-        inv_low[b, :size, :size] = low
+    loaded(4, 16, 17, 7)
     along_y = jnp.zeros((NQ, count_z), F32)
     for k in range(count_y):
         along_y = along_y + spready_ref[:, k : k + 1] * stiff_ref[0, k : k + 1, :]
@@ -305,16 +310,6 @@
     own_hot = (owner_ref[...] == iota((vertices, vertices), 0)).astype(F32).astype(BF16)
 
     wide = inv_high.shape[2]
-    pick = (
-        iota((vertices, wide), 0) == g * message + lax.rem(iota((vertices, wide), 1), message)
-    ).astype(F32).astype(BF16)
-    shape = (groups * 8, wide)
-    row, lane = iota(shape, 0), iota(shape, 1)
-    pick_mask = (
-        (lane // block == lax.rem(row, 8))
-        & (lax.rem(lane, block) // message == lax.rem(row // 8, per_block))
-        & (lane < size)
-    )
     owner_rows = -(-groups // 8) * 8
 
     def choices(owner, group):
@@ -322,8 +317,6 @@
         rows = iota((wide, vertices), 0)
         chosen = jnp.concatenate([rows == c * block + place for c in range(3)], axis=1)
         return chosen.astype(F32).astype(BF16), iota((owner_rows, vertices), 0) == owner // message
-
-    own_choices = choices(owner_ref[...], g)
 
     def gradients(own, beyond, to_b, to_z):
         parts = []
@@ -432,19 +425,26 @@
     def widened(own, beyond):
         return jnp.concatenate([jnp.concatenate([own[c], beyond[c]], axis=0) for c in range(3)], axis=1)
 
-    loaded(*[i for i in range(INPUTS) if i not in (3, 5, 1, 0, 8, 6, 4, 16, 17)])
+    loaded(2, 9, 10, 11, 12, 13)
     own_rhs = [rhs_ref[c].reshape(4 * ny, lanes) for c in range(3)]
 
-    copy_state.wait_recv()
+    @pl.when(jnp.logical_not(is_last))
+    def _():
+        halo[0].wait_recv()
+
     beyond_state = [jnp.where(is_last, 0.0, halo_state[c]) for c in range(3)]
     gradients(state_z, along_z(beyond_state), gsb, gsz)
-    copy_halo.wait_recv()
-    beyond_direction = [jnp.where(is_last, 0.0, halo_rx[c * ny : (c + 1) * ny, :]) for c in range(3)]
-    keep_right = halo_rx[3 * ny : 4 * ny, :]
-    owner_right = halo_rx[4 * ny : 4 * ny + 1, :].astype(jnp.int32)
+
+    @pl.when(jnp.logical_not(is_last))
+    def _():
+        for copy in halo[1:]:
+            copy.wait_recv()
+
+    keep_right = jnp.where(is_last, 0.0, keep_of(clamp_column(halo_clamp, 0)))
+    beyond_direction = [jnp.where(is_last, 0.0, keep_right * halo_rx[c]) for c in range(3)]
+    owner_right = halo_owner[...]
     right_hot = (owner_right == iota((vertices, vertices), 0)).astype(F32).astype(BF16)
     gradients(direction_z, along_z(beyond_direction), gvb, gvz)
-    right_choices = choices(owner_right, g_right)
     fluxes(True)
     image = divergence()
 
@@ -478,9 +478,34 @@
             (p, m_right),
         ).start()
 
-    each(0, groups, send_next)
+    @pl.when(jnp.logical_not(is_last))
+    def _():
+        each(0, groups, send_next)
+
     each(1, groups, send_own)
     sums_rx[g] = sums_tx[0]
+
+    @pl.when(at_start)
+    def _():
+        sums_rx[groups] = jnp.zeros((8, vertices), F32)
+
+    loaded(6)
+    inv_high[...] = jnp.zeros_like(inv_high)
+    inv_low[...] = jnp.zeros_like(inv_low)
+    for b in range(blocks):
+        high, low = split(inverse_ref[0, b])
+        inv_high[b, :size, :size] = high
+        inv_low[b, :size, :size] = low
+    pick = (
+        iota((vertices, wide), 0) == g * message + lax.rem(iota((vertices, wide), 1), message)
+    ).astype(F32).astype(BF16)
+    shape = (groups * 8, wide)
+    row, lane = iota(shape, 0), iota(shape, 1)
+    pick_mask = (
+        (lane // block == lax.rem(row, 8))
+        & (lax.rem(lane, block) // message == lax.rem(row // 8, per_block))
+        & (lane < size)
+    )
 
     def got_own(d):
         p = lax.rem(g + d, groups)
@@ -488,14 +513,19 @@
             sums_tx.at[0, pl.ds(0, 4)], sums_rx.at[p, pl.ds(0, 4)], sums_send.at[d], sums_recv.at[p], (p, m)
         ).wait()
 
-    def got_next(p):
-        remote(
+    def next_copy(p):
+        return remote(
             sums_tx.at[1, pl.ds(0, 4)],
             sums_rx.at[groups + p, pl.ds(0, 4)],
             sums_send.at[groups + p],
             sums_recv.at[groups + p],
             right,
-        ).wait()
+        )
+
+    def got_next(p):
+        @pl.when(jnp.logical_not(at_start & (p == 0)))
+        def _():
+            next_copy(p).wait_recv()
 
     each(1, groups, got_own)
     each(0, groups, got_next)
@@ -517,20 +547,31 @@
             solved_tx.at[p // per_block], solved_rx.at[g], solved_send.at[d], solved_recv.at[g], (p, m)
         ).start()
 
-    def return_left(d):
+    def left_copy(d):
         p = lax.rem(g + d, groups)
         before = lax.rem(p + groups - at_start.astype(jnp.int32), groups)
-        remote(
+        return p, remote(
             solved_tx.at[p // per_block],
             solved_rx.at[groups + g],
             solved_send.at[groups + d],
             solved_recv.at[groups + g],
             (before, m_left),
-        ).start()
+        )
+
+    def return_left(d):
+        p, copy = left_copy(d)
+        pl.when(jnp.logical_not(at_start & (p == 0)))(copy.start)
+
+    def left_sent(d):
+        p, copy = left_copy(d)
+        pl.when(jnp.logical_not(at_start & (p == 0)))(copy.wait_send)
 
     each(0, groups, return_left)
     each(1, groups, return_own)
     solved_rx[g] = solved_tx[g // per_block]
+    loaded(14, 15)
+    own_choices = choices(owner_ref[...], g)
+    right_choices = choices(owner_right, g_right)
 
     def back_own(d):
         p = lax.rem(g + d, groups)
@@ -539,10 +580,14 @@
     def back_next(p):
         remote(
             solved_tx.at[0], solved_rx.at[groups + p], solved_send.at[groups + p], solved_recv.at[groups + p], right
-        ).wait()
+        ).wait_recv()
 
     each(1, groups, back_own)
-    each(0, groups, back_next)
+
+    @pl.when(jnp.logical_not(is_last))
+    def _():
+        each(0, groups, back_next)
+
 
     def corrections(start, chosen, mask):
         at_row = iota((owner_rows, wide), 0)
@@ -580,47 +625,58 @@
     copy_layer = remote(
         last_tx.at[pl.ds(0, 3 * ny)], last_rx.at[pl.ds(0, 3 * ny)], last_send.at[0], last_recv.at[0], right
     )
-    copy_layer.start()
+    pl.when(jnp.logical_not(is_last))(copy_layer.start)
     own_last, beyond_last = settle(image, new_direction)
     low_sums, high_sums = restrict(widened(own_last, beyond_last))
     last_tx[3 * ny :, :] = high_sums
     copy_sums = remote(
         last_tx.at[pl.ds(3 * ny, 8)], last_rx.at[pl.ds(3 * ny, 8)], last_send.at[1], last_recv.at[1], right
     )
-    copy_sums.start()
+    pl.when(jnp.logical_not(is_last))(copy_sums.start)
     for c in range(3):
         residual_ref[c, 1:] = own_last[c][ny:].reshape(3, ny, lanes)
     store_rest = pltpu.make_async_copy(residual_ref.at[:, 1:], outputs[1].at[:, 1:], store_sem.at[1])
     store_rest.start()
-    copy_layer.wait_recv()
+    pl.when(jnp.logical_not(is_first))(copy_layer.wait_recv)
     for c in range(3):
         arrived = jnp.where(is_first, 0.0, last_rx[c * ny : (c + 1) * ny, :])
         residual_ref[c, 0] = own_last[c][:ny] - keep[:ny] * arrived
     store_first = pltpu.make_async_copy(residual_ref.at[:, 0], outputs[1].at[:, 0], store_sem.at[2])
     store_first.start()
-    copy_sums.wait_recv()
+    pl.when(jnp.logical_not(is_first))(copy_sums.wait_recv)
     total = low_sums + jnp.where(is_first, 0.0, last_rx[3 * ny :, :])
     for c in range(3):
         for k in range(count_y):
             coarse_ref[c, 0, k : k + 1, :] = total[c : c + 1, k * count_z : (k + 1) * count_z]
     store_coarse = pltpu.make_async_copy(coarse_ref, outputs[2], store_sem.at[3])
     store_coarse.start()
-    store_new.wait()
-    store_rest.wait()
-    store_first.wait()
-    store_coarse.wait()
-    copy_state.wait_send()
-    copy_halo.wait_send()
-    copy_layer.wait_send()
-    copy_sums.wait_send()
-
-
-def write_out(new, residual, coarse, new_out, residual_out, coarse_out, sems):
-    pairs = ((new, new_out), (residual, residual_out), (coarse, coarse_out))
-    copies = [pltpu.make_async_copy(a, b, sems.at[i]) for i, (a, b) in enumerate(pairs)]
-    for copy in copies:
+    each(0, groups, left_sent)
+
+    @pl.when(jnp.logical_not(is_first))
+    def _():
+        for copy in halo:
+            copy.wait_send()
+
+    @pl.when(jnp.logical_not(is_last))
+    def _():
+        each(0, groups, lambda p: next_copy(p).wait_send())
+        copy_layer.wait_send()
+        copy_sums.wait_send()
+
+    for copy in (store_new, store_rest, store_first, store_coarse):
+        copy.wait()
+
+
+def write_out(*refs):
+    sources, targets, held, sems = refs[:3], refs[3:6], refs[6:9], refs[9]
+    loads = [pltpu.make_async_copy(a, b, sems.at[i]) for i, (a, b) in enumerate(zip(sources, held))]
+    stores = [pltpu.make_async_copy(a, b, sems.at[3 + i]) for i, (a, b) in enumerate(zip(held, targets))]
+    for copy in loads:
         copy.start()
-    for copy in copies:
+    for load, store in zip(loads, stores):
+        load.wait()
+        store.start()
+    for copy in stores:
         copy.wait()
 
 
@@ -631,23 +687,23 @@
     blocks, size = coarse_inverse.shape[1:3]
     wide = -(-size // 128) * 128
     vertices = count_y * count_z
+    results = tuple(
+        jax.ShapeDtypeStruct(t, F32) for t in (state.shape, state.shape, (3, 1, count_y, count_z))
+    )
     operands = [state, direction, rhs, clamp, stiffness, coarse_owner, coarse_inverse, *tables]
     new, residual, coarse = pl.pallas_call(
         functools.partial(kernel, groups, members),
-        out_shape=(
-            jax.ShapeDtypeStruct(state.shape, F32),
-            jax.ShapeDtypeStruct(state.shape, F32),
-            jax.ShapeDtypeStruct((3, 1, count_y, count_z), F32),
-        ),
+        out_shape=results,
         in_specs=[pl.BlockSpec(memory_space=pl.ANY)] * INPUTS,
         out_specs=[pl.BlockSpec(memory_space=pl.ANY)] * 3,
         scratch_shapes=[pltpu.VMEM(t.shape, t.dtype) for t in operands]
-        + [pltpu.VMEM(t.shape, F32) for t in (state, state, jnp.zeros((3, 1, count_y, count_z), F32))]
+        + [pltpu.VMEM(t.shape, F32) for t in results]
         + [pltpu.VMEM(t.shape, BF16) for t in tables[:9]]
         + [
-            pltpu.VMEM((4 * ny + 8, nz), F32),
+            pltpu.VMEM(clamp.shape, jnp.int32),
+            pltpu.VMEM(coarse_owner.shape, jnp.int32),
             pltpu.VMEM((3, ny, nz), F32),
-            pltpu.VMEM((4 * ny + 8, nz), F32),
+            pltpu.VMEM((3, ny, nz), F32),
             pltpu.VMEM((2, 8, vertices), F32),
             pltpu.VMEM((2 * groups, 8, vertices), F32),
             pltpu.VMEM((blocks, 1, wide), F32),
@@ -667,8 +723,8 @@
             pltpu.VMEM((6 * NQ, 256), BF16),
             pltpu.VMEM((3 * NQ, 256), BF16),
             pltpu.VMEM((3 * NQ, 256), BF16),
-            pltpu.SemaphoreType.DMA((2,)),
-            pltpu.SemaphoreType.DMA((2,)),
+            pltpu.SemaphoreType.DMA((4,)),
+            pltpu.SemaphoreType.DMA((4,)),
             pltpu.SemaphoreType.DMA((2 * groups,)),
             pltpu.SemaphoreType.DMA((2 * groups,)),
             pltpu.SemaphoreType.DMA((2 * groups,)),
@@ -684,10 +740,10 @@
     )(*operands)
     return pl.pallas_call(
         write_out,
-        out_shape=tuple(jax.ShapeDtypeStruct(t.shape, F32) for t in (new, residual, coarse)),
+        out_shape=results,
         in_specs=[pl.BlockSpec(memory_space=pl.ANY)] * 3,
         out_specs=[pl.BlockSpec(memory_space=pl.ANY)] * 3,
-        scratch_shapes=[pltpu.SemaphoreType.DMA((3,))],
+        scratch_shapes=[pltpu.VMEM(t.shape, F32) for t in results] + [pltpu.SemaphoreType.DMA((6,))],
         compiler_params=pltpu.CompilerParams(vmem_limit_bytes=56 * 1024 * 1024),
     )(new, residual, coarse)
 

time: 38.7 us -> 28.9 us (0.75)
  the two profiles are of different devices: /device:TPU:0 before, /device:TPU:8 now
where the time goes in v3:
time: 28.9 us; the launch traced here: 28.8 us
  Pallas kernels  28.1 us (97%)
  between operations  0.64 us (2%)
    pallas_call x1, Pallas kernels, shards(): pl.pallas_call(functools.partial(kernel, groups, members), out_shape=resu...  26.5 us
    pallas_call x1, Pallas kernels, shards(): pl.pallas_call(write_out, out_shape=results, in_specs=[pl.BlockSpec(memor...  1.63 us

profile of v3, /device:TPU:8, one launch (start us, length us, event | category | flops | bytes accessed | tf_op | source)
XLA Modules:
  0.0 28.8 jit_solution(14090395031549987810)
XLA Ops:
  0.6 26.5 %shard_map.193 = (f32[3,4,16,128]{3,2,1,0:T(8,128)}, f32[3,4,16,128]{3,2,1,0:T(8,128)}, f32[3,1,4,32]{3,2,1,0:T(4,128)}) custom-call(f32[3,4,16,128]{3,2,1,0:T(8,128)} %refs_0_.1, f32[3,4,16,128]{3,2,1,0:T(8,128)} %refs_1_.1, f32[3,4,16,128]{3,2,1,0:T(8,128)} %refs_2_.1, s32[4,16]{1,0:T(4,128)} %refs_3_.1, f32[1,4,32]{2,1,0:T(4,128)} %refs_4_.1, ...), custom_call_target="tpu_custom_call" | custom-call | tf_op jit(solution)/shard_map/pallas_call | solution.py:694
  27.1 1.6 %shard_map.194 = (f32[3,4,16,128]{3,2,1,0:T(8,128)}, f32[3,4,16,128]{3,2,1,0:T(8,128)}, f32[3,1,4,32]{3,2,1,0:T(4,128)}) custom-call(f32[3,4,16,128]{3,2,1,0:T(8,128)} %get-tuple-element.6.refs_0_, f32[3,4,16,128]{3,2,1,0:T(8,128)} %get-tuple-element.7.refs_1_, f32[3,1,4,32]{3,2,1,0:T(4,128)} %get-tuple-element.8.refs_2_), custom_call_target="tpu_custom_call" | custom-call | tf_op jit(solution)/shard_map/pallas_call | solution.py:741

commit v4 on v3

--- a/solution.py
+++ b/solution.py
@@ -79,11 +79,6 @@
 def left_table(table):
     high, low = halves(table)
     return padded(np.concatenate([high, high, low], axis=1), 1, 128)
-
-
-def right_table(table):
-    high, low = halves(table)
-    return np.concatenate([high, high, low], axis=0)
 
 
 def constant_tables(count_y, count_z):
@@ -108,13 +103,13 @@
     spread_z = padded(np.kron(np.eye(count_z), weights[None]), 1, 256)
     return (
         left_table(cross),
-        right_table(np.concatenate([bz.T, dz.T], axis=1)),
-        np.concatenate(halves(bz), axis=1),
-        np.concatenate(halves(dz), axis=1),
+        np.concatenate([bz.T, dz.T], axis=1),
+        bz,
+        dz,
         left_table(cross.T),
         left_table(hats),
-        right_table(tiled.T),
-        right_table(tiled),
+        tiled.T,
+        tiled,
         left_table(hats.T),
         spread_y.astype(np.float32),
         spread_z.astype(np.float32),
@@ -244,7 +239,7 @@
     each(0, groups, lambda d: greet(lax.rem(g_right + d, groups), m_right))
     each(1, groups, lambda d: greet(lax.rem(g + d, groups), m))
     loads = [pltpu.make_async_copy(a, b, load_sem.at[i]) for i, (a, b) in enumerate(zip(sources, local))]
-    order = [3, 5, 1, 0, 6, 4, 16, 17, 8, 7]
+    order = [3, 5, 1, 0, 8, 4, 16, 17, 7, 9, 10, 11, 2, 12, 13, 6]
     for i in order + [i for i in range(INPUTS) if i not in order]:
         loads[i].start()
 
@@ -252,7 +247,18 @@
         for i in which:
             loads[i].wait()
             if 7 <= i < 16:
-                narrow[i - 7][...] = local[i][...].astype(BF16)
+                target = narrow[i - 7]
+                rows, columns = local[i].shape
+                if target.shape == local[i].shape:
+                    target[...] = local[i][...].astype(BF16)
+                    continue
+                high, low = split(local[i][...])
+                target[:rows, :columns] = high
+                if target.shape[0] == rows:
+                    target[:, columns:] = low
+                else:
+                    target[rows : 2 * rows, :] = high
+                    target[2 * rows :, :] = low
 
     pl.semaphore_wait(barrier, 3 * groups - 1)
 
@@ -299,8 +305,7 @@
     loaded(0, 8)
     own_state = [state_ref[c].reshape(4 * ny, lanes) for c in range(3)]
     own_direction = [direction_ref[c].reshape(4 * ny, lanes) for c in range(3)]
-    state_z = along_z(own_state)
-    direction_z = along_z([keep * t for t in own_direction])
+    own_z = along_z(own_state + [keep * t for t in own_direction])
     sums_rx[:, 4:, :] = jnp.zeros((2 * groups, 4, vertices), F32)
     loaded(4, 16, 17, 7)
     along_y = jnp.zeros((NQ, count_z), F32)
@@ -318,22 +323,12 @@
         chosen = jnp.concatenate([rows == c * block + place for c in range(3)], axis=1)
         return chosen.astype(F32).astype(BF16), iota((owner_rows, vertices), 0) == owner // message
 
-    def gradients(own, beyond, to_b, to_z):
-        parts = []
-        for first in (0, 256):
-            columns = [
-                jnp.concatenate(
-                    [
-                        own[c * 4 * ny : (c + 1) * 4 * ny, first : first + 256],
-                        beyond[c * ny : (c + 1) * ny, first : first + 256],
-                    ],
-                    axis=0,
-                )
-                for c in range(3)
-            ]
-            parts.append(jnp.concatenate(columns, axis=1))
-        to_b[...] = times_left(cross_ref[: 2 * NQ, :], parts[0])
-        to_z[...] = times_left(cross_ref[2 * NQ :, :], parts[1])
+    def gradients(columns, targets):
+        for first, rows, place in ((0, pl.ds(0, 2 * NQ), 0), (256, pl.ds(2 * NQ, NQ), 1)):
+            wide_field = jnp.concatenate([t[:, first : first + 256] for t in columns], axis=1)
+            result = times_left(cross_ref[rows, :], wide_field)
+            for i, target in enumerate(targets):
+                target[place][...] = result[:, i * 768 : (i + 1) * 768]
 
     def load_change(from_b, from_z, r, half):
         change = []
@@ -430,21 +425,20 @@
 
     @pl.when(jnp.logical_not(is_last))
     def _():
-        halo[0].wait_recv()
+        for copy in halo:
+            copy.wait_recv()
 
     beyond_state = [jnp.where(is_last, 0.0, halo_state[c]) for c in range(3)]
-    gradients(state_z, along_z(beyond_state), gsb, gsz)
-
-    @pl.when(jnp.logical_not(is_last))
-    def _():
-        for copy in halo[1:]:
-            copy.wait_recv()
-
     keep_right = jnp.where(is_last, 0.0, keep_of(clamp_column(halo_clamp, 0)))
     beyond_direction = [jnp.where(is_last, 0.0, keep_right * halo_rx[c]) for c in range(3)]
     owner_right = halo_owner[...]
     right_hot = (owner_right == iota((vertices, vertices), 0)).astype(F32).astype(BF16)
-    gradients(direction_z, along_z(beyond_direction), gvb, gvz)
+    beyond_z = along_z(beyond_state + beyond_direction)
+    columns = [
+        jnp.concatenate([own_z[i * 4 * ny : (i + 1) * 4 * ny], beyond_z[i * ny : (i + 1) * ny]], axis=0)
+        for i in range(6)
+    ]
+    gradients(columns, ((gsb, gsz), (gvb, gvz)))
     fluxes(True)
     image = divergence()
 
@@ -462,18 +456,24 @@
     sums_tx[0] = stacked_exact(low_sums, own_hot, dot_nt)
     sums_tx[1] = stacked_exact(high_sums, right_hot, dot_nt)
 
-    def send_own(d):
-        p = lax.rem(g + d, groups)
-        remote(
-            sums_tx.at[0, pl.ds(0, 4)], sums_rx.at[g, pl.ds(0, 4)], sums_send.at[d], sums_recv.at[g], (p, m)
-        ).start()
-
-    def send_next(d):
-        p = lax.rem(g_right + d, groups)
+    def far(i):
+        return jnp.where(g >= groups // 2, i, groups - 1 - i)
+
+    def send_own(i):
+        p = far(i)
+
+        @pl.when(p != g)
+        def _():
+            remote(
+                sums_tx.at[0, pl.ds(0, 4)], sums_rx.at[g, pl.ds(0, 4)], sums_send.at[p], sums_recv.at[g], (p, m)
+            ).start()
+
+    def send_next(i):
+        p = far(i)
         remote(
             sums_tx.at[1, pl.ds(0, 4)],
             sums_rx.at[groups + g_right, pl.ds(0, 4)],
-            sums_send.at[groups + d],
+            sums_send.at[groups + p],
             sums_recv.at[groups + g_right],
             (p, m_right),
         ).start()
@@ -482,7 +482,7 @@
     def _():
         each(0, groups, send_next)
 
-    each(1, groups, send_own)
+    each(0, groups, send_own)
     sums_rx[g] = sums_tx[0]
 
     @pl.when(at_start)
@@ -510,7 +510,7 @@
     def got_own(d):
         p = lax.rem(g + d, groups)
         remote(
-            sums_tx.at[0, pl.ds(0, 4)], sums_rx.at[p, pl.ds(0, 4)], sums_send.at[d], sums_recv.at[p], (p, m)
+            sums_tx.at[0, pl.ds(0, 4)], sums_rx.at[p, pl.ds(0, 4)], sums_send.at[p], sums_recv.at[p], (p, m)
         ).wait()
 
     def next_copy(p):
@@ -541,19 +541,22 @@
         both = dot_nt(jnp.concatenate([high, low], axis=0), inv_high[b])
         solved_tx[b] = (both[:1] + both[8:9]) + dot_nt(jnp.concatenate([high, high], axis=0), inv_low[b])[:1]
 
-    def return_own(d):
-        p = lax.rem(g + d, groups)
-        remote(
-            solved_tx.at[p // per_block], solved_rx.at[g], solved_send.at[d], solved_recv.at[g], (p, m)
-        ).start()
-
-    def left_copy(d):
-        p = lax.rem(g + d, groups)
+    def return_own(i):
+        p = far(i)
+
+        @pl.when(p != g)
+        def _():
+            remote(
+                solved_tx.at[p // per_block], solved_rx.at[g], solved_send.at[p], solved_recv.at[g], (p, m)
+            ).start()
+
+    def left_copy(i):
+        p = far(i)
         before = lax.rem(p + groups - at_start.astype(jnp.int32), groups)
         return p, remote(
             solved_tx.at[p // per_block],
             solved_rx.at[groups + g],
-            solved_send.at[groups + d],
+            solved_send.at[groups + p],
             solved_recv.at[groups + g],
             (before, m_left),
         )
@@ -567,7 +570,7 @@
         pl.when(jnp.logical_not(at_start & (p == 0)))(copy.wait_send)
 
     each(0, groups, return_left)
-    each(1, groups, return_own)
+    each(0, groups, return_own)
     solved_rx[g] = solved_tx[g // per_block]
     loaded(14, 15)
     own_choices = choices(owner_ref[...], g)
@@ -575,7 +578,7 @@
 
     def back_own(d):
         p = lax.rem(g + d, groups)
-        remote(solved_tx.at[0], solved_rx.at[p], solved_send.at[d], solved_recv.at[p], (p, m)).wait()
+        remote(solved_tx.at[0], solved_rx.at[p], solved_send.at[p], solved_recv.at[p], (p, m)).wait()
 
     def back_next(p):
         remote(
@@ -617,7 +620,8 @@
     store_new = pltpu.make_async_copy(new_ref, outputs[0], store_sem.at[0])
     store_new.start()
     beyond_new = [jnp.where(is_last, 0.0, t) for t in beyond_new]
-    gradients(along_z([keep * t for t in new_direction]), along_z(beyond_new), gvb, gvz)
+    whole_z = along_z([t for c in range(3) for t in (keep * new_direction[c], beyond_new[c])])
+    gradients([whole_z[c * 5 * ny : (c + 1) * 5 * ny] for c in range(3)], ((gvb, gvz),))
     fluxes(False)
     image = divergence()
     for c in range(3):
@@ -698,7 +702,10 @@
         out_specs=[pl.BlockSpec(memory_space=pl.ANY)] * 3,
         scratch_shapes=[pltpu.VMEM(t.shape, t.dtype) for t in operands]
         + [pltpu.VMEM(t.shape, F32) for t in results]
-        + [pltpu.VMEM(t.shape, BF16) for t in tables[:9]]
+        + [
+            pltpu.VMEM((t.shape[0] * by_rows, t.shape[1] * by_columns), BF16)
+            for t, by_rows, by_columns in zip(tables, (1, 3, 1, 1, 1, 1, 3, 3, 1), (1, 1, 2, 2, 1, 1, 1, 1, 1))
+        ]
         + [
             pltpu.VMEM(clamp.shape, jnp.int32),
             pltpu.VMEM(coarse_owner.shape, jnp.int32),

time: 28.9 us -> 28.8 us (level)
  no operation moved by 1% of the time
where the time goes in v4:
time: 28.8 us; the launch traced here: 28.6 us
  Pallas kernels  28 us (97%)
  between operations  0.64 us (2%)
    pallas_call x1, Pallas kernels, shards(): pl.pallas_call(functools.partial(kernel, groups, members), out_shape=resu...  26.3 us
    pallas_call x1, Pallas kernels, shards(): pl.pallas_call(write_out, out_shape=results, in_specs=[pl.BlockSpec(memor...  1.63 us

profile of v4, /device:TPU:8, one launch (start us, length us, event | category | flops | bytes accessed | tf_op | source)
XLA Modules:
  0.0 28.6 jit_solution(10282062671617969913)
XLA Ops:
  0.6 26.3 %shard_map.193 = (f32[3,4,16,128]{3,2,1,0:T(8,128)}, f32[3,4,16,128]{3,2,1,0:T(8,128)}, f32[3,1,4,32]{3,2,1,0:T(4,128)}) custom-call(f32[3,4,16,128]{3,2,1,0:T(8,128)} %refs_0_.1, f32[3,4,16,128]{3,2,1,0:T(8,128)} %refs_1_.1, f32[3,4,16,128]{3,2,1,0:T(8,128)} %refs_2_.1, s32[4,16]{1,0:T(4,128)} %refs_3_.1, f32[1,4,32]{2,1,0:T(4,128)} %refs_4_.1, ...), custom_call_target="tpu_custom_call" | custom-call | tf_op jit(solution)/shard_map/pallas_call | solution.py:698
  27.0 1.6 %shard_map.194 = (f32[3,4,16,128]{3,2,1,0:T(8,128)}, f32[3,4,16,128]{3,2,1,0:T(8,128)}, f32[3,1,4,32]{3,2,1,0:T(4,128)}) custom-call(f32[3,4,16,128]{3,2,1,0:T(8,128)} %get-tuple-element.6.refs_0_, f32[3,4,16,128]{3,2,1,0:T(8,128)} %get-tuple-element.7.refs_1_, f32[3,1,4,32]{3,2,1,0:T(4,128)} %get-tuple-element.8.refs_2_), custom_call_target="tpu_custom_call" | custom-call | tf_op jit(solution)/shard_map/pallas_call | solution.py:748

commit v5 on v4

--- a/solution.py
+++ b/solution.py
@@ -390,7 +390,7 @@
                             fzl[place, s] = low
             return carry
 
-        lax.fori_loop(0, NQ // 16, body, 0)
+        lax.fori_loop(0, NQ // 16, body, 0, unroll=True)
 
     def divergence():
         both_b = dot(fbh[...], bzt_ref[...])

time: 28.8 us -> 28.6 us (level)
  no operation moved by 1% of the time
where the time goes in v5:
time: 28.6 us; the launch traced here: 28.4 us
  Pallas kernels  27.8 us (97%)
  between operations  0.64 us (2%)
    pallas_call x1, Pallas kernels, shards(): pl.pallas_call(functools.partial(kernel, groups, members), out_shape=resu...  26.2 us
    pallas_call x1, Pallas kernels, shards(): pl.pallas_call(write_out, out_shape=results, in_specs=[pl.BlockSpec(memor...  1.63 us

profile of v5, /device:TPU:8, one launch (start us, length us, event | category | flops | bytes accessed | tf_op | source)
XLA Modules:
  0.0 28.4 jit_solution(10774237309718714633)
XLA Ops:
  0.6 26.2 %shard_map.193 = (f32[3,4,16,128]{3,2,1,0:T(8,128)}, f32[3,4,16,128]{3,2,1,0:T(8,128)}, f32[3,1,4,32]{3,2,1,0:T(4,128)}) custom-call(f32[3,4,16,128]{3,2,1,0:T(8,128)} %refs_0_.1, f32[3,4,16,128]{3,2,1,0:T(8,128)} %refs_1_.1, f32[3,4,16,128]{3,2,1,0:T(8,128)} %refs_2_.1, s32[4,16]{1,0:T(4,128)} %refs_3_.1, f32[1,4,32]{2,1,0:T(4,128)} %refs_4_.1, ...), custom_call_target="tpu_custom_call" | custom-call | tf_op jit(solution)/shard_map/pallas_call | solution.py:698
  26.8 1.6 %shard_map.194 = (f32[3,4,16,128]{3,2,1,0:T(8,128)}, f32[3,4,16,128]{3,2,1,0:T(8,128)}, f32[3,1,4,32]{3,2,1,0:T(4,128)}) custom-call(f32[3,4,16,128]{3,2,1,0:T(8,128)} %get-tuple-element.6.refs_0_, f32[3,4,16,128]{3,2,1,0:T(8,128)} %get-tuple-element.7.refs_1_, f32[3,1,4,32]{3,2,1,0:T(4,128)} %get-tuple-element.8.refs_2_), custom_call_target="tpu_custom_call" | custom-call | tf_op jit(solution)/shard_map/pallas_call | solution.py:748
